TPU v7x, 32 devices: a whole 2x2x4 slice. The times are simulated.
32 devices in a mesh: section: 2 (over core), dp: 16 (over z, y, x).
Axes of the slice: x: 2, y: 2, z: 4, core: 2. Of those that a mesh axis runs over, the one named last changes fastest.
Arguments:
- inputs: bfloat16 [16384, 1024], P('dp'), may hold values from -6 to 6
- qkv_weight: float32 [2, 1024, 3072], P('section', 'dp'), may hold values from -0.1875 to 0.1875
- out_weight: float32 [2, 1024, 1024], P('section', 'dp'), may hold values from -1.5 to 1.5
- cross_query: float32 [2, 1024, 1024], P('section', 'dp'), may hold values from -0.1875 to 0.1875
- cross_kv: float32 [2, 1024, 2048], P('section', 'dp'), may hold values from -0.1875 to 0.1875
- cross_out: float32 [2, 1024, 1024], P('section', 'dp'), may hold values from -1.5 to 1.5
- ffn_in: float32 [2, 1024, 4096], P('section', 'dp'), may hold values from -0.1875 to 0.1875
- ffn_out: float32 [2, 4096, 1024], P('section', 'dp'), may hold values from -0.21875 to 0.21875
- norm_gains: float32 [2, 3, 1024], P('section', None, 'dp'), may hold values from 0.1 to 1.9
- type_embed: float32 [2, 2, 1024], P('section', None, 'dp'), may hold values from -3 to 3
- encoder: bfloat16 [2, 16384, 1024], P('section', 'dp'), may hold values from -6 to 6
- lengths: int32 [32], P('dp'), may hold values from 128 to 512, as said below
- seq_types: int32 [32], P('dp'), may hold values from 0 to 1
- enc_mask: int32 [32, 512], P('dp'), may hold values from 0 to 1, as said below
- cotangent: bfloat16 [2, 16384, 1024], P('section', 'dp'), may hold values from -6 to 6
Outputs:
- layer_outputs: bfloat16 [2, 16384, 1024], P('section', 'dp')
- input_grads: bfloat16 [2, 16384, 1024], P('section', 'dp')
- encoder_grads: bfloat16 [2, 16384, 1024], P('section', 'dp')
- qkv_grad: float32 [2, 1024, 3072], P('section', 'dp')
- out_grad: float32 [2, 1024, 1024], P('section', 'dp')
- cross_query_grad: float32 [2, 1024, 1024], P('section', 'dp')
- cross_kv_grad: float32 [2, 1024, 2048], P('section', 'dp')
- cross_out_grad: float32 [2, 1024, 1024], P('section', 'dp')
- ffn_in_grad: float32 [2, 1024, 4096], P('section', 'dp')
- ffn_out_grad: float32 [2, 4096, 1024], P('section', 'dp')
- gains_grad: float32 [2, 3, 1024], P('section', None, 'dp')
- embed_grad: float32 [2, 2, 1024], P('section', None, 'dp')
Inputs may be any that keep to these rules, and one draw needn't show every extreme that they name: `lengths`: some sequence has exactly 512 valid positions. `enc_mask`: each row is ones over its first frames and zeros after them, with at least 128 ones; some row is all ones.
All inputs are finite; a program needn't handle non-finite values.
Results may differ from a plain program's by a relative error of at most 0.018.
Values may be sent and summed in bfloat16 or wider, within the bound.
A program may use at most 768 MiB of HBM per device.

v0:
```python
import jax
import jax.numpy as jnp
from jax import lax
from jax.sharding import PartitionSpec as P

HEADS = 16
MICRO = 2


EPS = 1e-05
NEG = -1e30


def from_behind(block, axis, distance):
    devices = range(lax.axis_size(axis))
    route = [(i - distance, i) for i in devices if i - distance in devices]
    return lax.ppermute(block, axis, route)


def norm_rows(h, gain):
    mean = jnp.mean(h, -1, keepdims=True)
    cent = h - mean
    var = jnp.mean(cent * cent, -1, keepdims=True)
    return cent * lax.rsqrt(var + EPS) * gain


def norm_back(h, gain, grad):
    _, pull = jax.vjp(norm_rows, h, gain)
    return pull(grad)


def gelu_exact(v):
    return jax.nn.gelu(v, approximate=False)


def matmul(left, right):
    return jnp.dot(left, right, preferred_element_type=jnp.float32)


def inner_rows(left, right):
    return lax.dot_general(
        left, right, (((0,), (0,)), ((), ())), preferred_element_type=jnp.float32
    )


def outer_cols(left, right):
    return lax.dot_general(
        left, right, (((1,), (1,)), ((), ())), preferred_element_type=jnp.float32
    )


def causal_allow(length, first, block, keys):
    query_pos = first + jnp.arange(block)[:, None]
    key_pos = jnp.arange(keys)[None, :]
    return (key_pos <= query_pos) & (key_pos < length)


def frame_allow(mask_row, first, block, keys):
    return jnp.broadcast_to(mask_row[None, :] == 1, (block, keys))


def split_heads(values, seqs):
    return values.reshape(seqs, values.shape[0] // seqs, HEADS, values.shape[1] // HEADS)


def attend_forward(query, keys, values, infos, allow_fn):
    seqs = infos.shape[0]
    query_h = split_heads(query, seqs)
    keys_h = split_heads(keys, seqs)
    values_h = split_heads(values, seqs)
    rows = query_h.shape[1]
    cols = keys_h.shape[1]
    scale = query_h.shape[3] ** (-0.5)
    block = min(512, rows)

    def one(args):
        query_s, keys_s, values_s, info = args
        outs = []
        sums = []
        for first in range(0, rows, block):
            allow = allow_fn(info, first, block, cols)
            scores = (
                jnp.einsum(
                    "qhd,khd->hqk",
                    query_s[first : first + block],
                    keys_s,
                    preferred_element_type=jnp.float32,
                )
                * scale
            )
            scores = jnp.where(allow[None], scores, NEG)
            top = jnp.max(scores, -1, keepdims=True)
            expo = jnp.exp(scores - top)
            total = jnp.sum(expo, -1, keepdims=True)
            probs = (expo / total).astype(jnp.bfloat16)
            outs.append(
                jnp.einsum("hqk,khd->qhd", probs, values_s, preferred_element_type=jnp.float32)
            )
            sums.append((top + jnp.log(total))[:, :, 0])
        return (jnp.concatenate(outs, 0), jnp.concatenate(sums, 1))

    result, lse = lax.map(one, (query_h, keys_h, values_h, infos))
    return (result.reshape(query.shape).astype(jnp.bfloat16), lse)


def attend_backward(query, keys, values, lse, grad_out, infos, allow_fn):
    seqs = infos.shape[0]
    query_h = split_heads(query, seqs)
    keys_h = split_heads(keys, seqs)
    values_h = split_heads(values, seqs)
    grad_h = split_heads(grad_out, seqs)
    rows = query_h.shape[1]
    cols = keys_h.shape[1]
    scale = query_h.shape[3] ** (-0.5)
    block = min(512, rows)

    def one(args):
        query_s, keys_s, values_s, sums, grad_s, info = args
        key_grad = jnp.zeros(keys_s.shape, jnp.float32)
        value_grad = jnp.zeros(values_s.shape, jnp.float32)
        query_grads = []
        for first in range(0, rows, block):
            allow = allow_fn(info, first, block, cols)
            query_b = query_s[first : first + block]
            grad_b = grad_s[first : first + block]
            scores = (
                jnp.einsum("qhd,khd->hqk", query_b, keys_s, preferred_element_type=jnp.float32)
                * scale
            )
            scores = jnp.where(allow[None], scores, NEG)
            probs = jnp.exp(scores - sums[:, first : first + block, None])
            value_grad = value_grad + jnp.einsum(
                "hqk,qhd->khd",
                probs.astype(jnp.bfloat16),
                grad_b,
                preferred_element_type=jnp.float32,
            )
            prob_grad = jnp.einsum(
                "qhd,khd->hqk", grad_b, values_s, preferred_element_type=jnp.float32
            )
            score_grad = (
                probs * (prob_grad - jnp.sum(prob_grad * probs, -1, keepdims=True))
            ).astype(jnp.bfloat16)
            query_grads.append(
                jnp.einsum("hqk,khd->qhd", score_grad, keys_s, preferred_element_type=jnp.float32)
                * scale
            )
            key_grad = (
                key_grad
                + jnp.einsum(
                    "hqk,qhd->khd", score_grad, query_b, preferred_element_type=jnp.float32
                )
                * scale
            )
        return (jnp.concatenate(query_grads, 0), key_grad, value_grad)

    query_grad, key_grad, value_grad = lax.map(one, (query_h, keys_h, values_h, lse, grad_h, infos))
    return (
        query_grad.reshape(query.shape),
        key_grad.reshape(keys.shape),
        value_grad.reshape(values.shape),
    )


def type_rows_of(types, rows):
    return jnp.repeat(types, rows // types.shape[0], total_repeat_length=rows)


def layer_forward(layer_in, weights, memory, lengths, types, mask):
    qkv_w, out_w, cq_w, ckv_w, cout_w, fin_w, fout_w, gains, embed = weights
    width = qkv_w.shape[0]
    gains = gains.astype(jnp.float32)
    embed = embed.astype(jnp.float32)
    is_speech = (type_rows_of(types, layer_in.shape[0]) == 1)[:, None]
    start = layer_in.astype(jnp.float32) + jnp.where(is_speech, embed[1], embed[0])
    qkv = matmul(norm_rows(start, gains[0]).astype(jnp.bfloat16), qkv_w).astype(jnp.bfloat16)
    ctx, lse_self = attend_forward(
        qkv[:, :width], qkv[:, width : 2 * width], qkv[:, 2 * width :], lengths, causal_allow
    )
    mid = start + matmul(ctx, out_w)
    cross_q = matmul(norm_rows(mid, gains[1]).astype(jnp.bfloat16), cq_w).astype(jnp.bfloat16)
    cross_mem = matmul(memory, ckv_w).astype(jnp.bfloat16)
    ctx_cross, lse_cross = attend_forward(
        cross_q, cross_mem[:, :width], cross_mem[:, width:], mask, frame_allow
    )
    late = mid + matmul(ctx_cross, cout_w)
    up = matmul(norm_rows(late, gains[2]).astype(jnp.bfloat16), fin_w)
    act = gelu_exact(up).astype(jnp.bfloat16)
    result = late + matmul(act, fout_w)
    saved = (start, qkv, lse_self, ctx, mid, cross_q, cross_mem, lse_cross, ctx_cross, late)
    return (result, saved)


def layer_backward(grad, saved, weights, memory, lengths, types, mask):
    qkv_w, out_w, cq_w, ckv_w, cout_w, fin_w, fout_w, gains, embed = weights
    width = qkv_w.shape[0]
    gains = gains.astype(jnp.float32)
    start, qkv, lse_self, ctx, mid, cross_q, cross_mem, lse_cross, ctx_cross, late = saved
    normed_late = norm_rows(late, gains[2]).astype(jnp.bfloat16)
    up = matmul(normed_late, fin_w)
    low_grad = grad.astype(jnp.bfloat16)
    act = gelu_exact(up).astype(jnp.bfloat16)
    g_fout = inner_rows(act, low_grad)
    d_act = outer_cols(low_grad, fout_w)
    _, gelu_pull = jax.vjp(gelu_exact, up)
    d_up = gelu_pull(d_act)[0].astype(jnp.bfloat16)
    g_fin = inner_rows(normed_late, d_up)
    d_late_part, g_gain2 = norm_back(late, gains[2], outer_cols(d_up, fin_w))
    d_late = grad + d_late_part
    low_late = d_late.astype(jnp.bfloat16)
    g_cout = inner_rows(ctx_cross, low_late)
    d_ctx_cross = outer_cols(low_late, cout_w).astype(jnp.bfloat16)
    dq_cross, dk_cross, dv_cross = attend_backward(
        cross_q,
        cross_mem[:, :width],
        cross_mem[:, width:],
        lse_cross,
        d_ctx_cross,
        mask,
        frame_allow,
    )
    d_cross_q = dq_cross.astype(jnp.bfloat16)
    d_cross_mem = jnp.concatenate([dk_cross, dv_cross], 1).astype(jnp.bfloat16)
    g_cq = inner_rows(norm_rows(mid, gains[1]).astype(jnp.bfloat16), d_cross_q)
    g_ckv = inner_rows(memory, d_cross_mem)
    d_memory = outer_cols(d_cross_mem, ckv_w)
    d_mid_part, g_gain1 = norm_back(mid, gains[1], outer_cols(d_cross_q, cq_w))
    d_mid = d_late + d_mid_part
    low_mid = d_mid.astype(jnp.bfloat16)
    g_out = inner_rows(ctx, low_mid)
    d_ctx = outer_cols(low_mid, out_w).astype(jnp.bfloat16)
    d_query, d_keys, d_values = attend_backward(
        qkv[:, :width],
        qkv[:, width : 2 * width],
        qkv[:, 2 * width :],
        lse_self,
        d_ctx,
        lengths,
        causal_allow,
    )
    d_qkv = jnp.concatenate([d_query, d_keys, d_values], 1).astype(jnp.bfloat16)
    g_qkv = inner_rows(norm_rows(start, gains[0]).astype(jnp.bfloat16), d_qkv)
    d_start_part, g_gain0 = norm_back(start, gains[0], outer_cols(d_qkv, qkv_w))
    d_start = d_mid + d_start_part
    is_speech = (type_rows_of(types, grad.shape[0]) == 1)[:, None]
    g_embed = jnp.stack(
        [
            jnp.sum(jnp.where(is_speech, 0.0, d_start), 0),
            jnp.sum(jnp.where(is_speech, d_start, 0.0), 0),
        ]
    )
    g_gains = jnp.stack([g_gain0, g_gain1, g_gain2])
    return (d_start, d_memory, (g_qkv, g_out, g_cq, g_ckv, g_cout, g_fin, g_fout, g_gains, g_embed))


def per_device(
    inputs,
    qkv_weight,
    out_weight,
    cross_query,
    cross_kv,
    cross_out,
    ffn_in,
    ffn_out,
    norm_gains,
    type_embed,
    encoder,
    lengths,
    seq_types,
    enc_mask,
    cotangent,
):
    half = jnp.bfloat16
    single = jnp.float32
    gathered = (
        lax.all_gather(qkv_weight.astype(half), "dp", axis=1, tiled=True),
        lax.all_gather(out_weight.astype(half), "dp", axis=1, tiled=True),
        lax.all_gather(cross_query.astype(half), "dp", axis=1, tiled=True),
        lax.all_gather(cross_kv.astype(half), "dp", axis=1, tiled=True),
        lax.all_gather(cross_out.astype(half), "dp", axis=1, tiled=True),
        lax.all_gather(ffn_in.astype(half), "dp", axis=1, tiled=True),
        lax.all_gather(ffn_out.astype(half), "dp", axis=1, tiled=True),
        lax.all_gather(norm_gains.astype(half), "dp", axis=2, tiled=True),
        lax.all_gather(type_embed.astype(half), "dp", axis=2, tiled=True),
    )
    weights = tuple((w[0] for w in gathered))
    section = lax.axis_index("section")
    micro = MICRO
    rows = inputs.shape[0] // micro
    seqs = lengths.shape[0] // micro
    frames = encoder.shape[1] // micro
    width = inputs.shape[1]
    memory_all = encoder[0]
    upstream = cotangent[0]
    per_seq = rows // seqs

    def pick(array, index, size):
        return lax.dynamic_slice_in_dim(array, index * size, size, 0)

    def meta_at(index):
        return (
            pick(memory_all, index, frames),
            pick(lengths, index, seqs),
            pick(seq_types, index, seqs),
            pick(enc_mask, index, seqs),
        )

    def run_forward(layer_in, meta):
        return layer_forward(layer_in, weights, meta[0], meta[1], meta[2], meta[3])

    def skip_forward(layer_in, meta):
        empty = (
            jnp.zeros((rows, width), single),
            jnp.zeros((rows, 3 * width), half),
            jnp.zeros((seqs, HEADS, per_seq), single),
            jnp.zeros((rows, width), half),
            jnp.zeros((rows, width), single),
            jnp.zeros((rows, width), half),
            jnp.zeros((frames, 2 * width), half),
            jnp.zeros((seqs, HEADS, per_seq), single),
            jnp.zeros((rows, width), half),
            jnp.zeros((rows, width), single),
        )
        return (jnp.zeros((rows, width), single), empty)

    held = jnp.zeros(((micro + 1) * rows, width), half)
    store = None
    sent = None
    for tick in range(micro + 1):
        index = tick - section
        valid = (index >= 0) & (index < micro)
        clipped = jnp.clip(index, 0, micro - 1)
        slot = jnp.where(valid, clipped, micro)
        own = pick(inputs, clipped, rows)
        if tick == 0:
            layer_in = own
        else:
            arrived = from_behind(sent, "section", 1)
            layer_in = jnp.where(section == 0, own, arrived)
        result, saved = lax.cond(valid, run_forward, skip_forward, layer_in, meta_at(clipped))
        sent = result.astype(half)
        if tick == 0:
            store = jax.tree.map(
                lambda value: jnp.zeros((micro + 1,) + value.shape, value.dtype), saved
            )
        store = jax.tree.map(
            lambda buffer, value: lax.dynamic_update_index_in_dim(buffer, value, slot, 0),
            store,
            saved,
        )
        held = lax.dynamic_update_slice_in_dim(held, sent, slot * rows, 0)
    regathered = (
        lax.all_gather(qkv_weight.astype(half), "dp", axis=1, tiled=True),
        lax.all_gather(out_weight.astype(half), "dp", axis=1, tiled=True),
        lax.all_gather(cross_query.astype(half), "dp", axis=1, tiled=True),
        lax.all_gather(cross_kv.astype(half), "dp", axis=1, tiled=True),
        lax.all_gather(cross_out.astype(half), "dp", axis=1, tiled=True),
        lax.all_gather(ffn_in.astype(half), "dp", axis=1, tiled=True),
        lax.all_gather(ffn_out.astype(half), "dp", axis=1, tiled=True),
        lax.all_gather(norm_gains.astype(half), "dp", axis=2, tiled=True),
        lax.all_gather(type_embed.astype(half), "dp", axis=2, tiled=True),
    )
    weights = tuple((w[0] for w in regathered))
    layer_weights = weights

    def run_backward(grad, saved, meta):
        return layer_backward(grad, saved, layer_weights, meta[0], meta[1], meta[2], meta[3])

    def skip_backward(grad, saved, meta):
        return (
            jnp.zeros((rows, width), single),
            jnp.zeros((frames, width), single),
            tuple((jnp.zeros(w.shape, single) for w in layer_weights)),
        )

    accum = tuple((jnp.zeros(w.shape, single) for w in layer_weights))
    given = jnp.zeros(((micro + 1) * rows, width), half)
    memory_grads = jnp.zeros(((micro + 1) * frames, width), half)
    returned = None
    for tick in range(micro + 1):
        index = micro - tick - section
        valid = (index >= 0) & (index < micro)
        clipped = jnp.clip(index, 0, micro - 1)
        slot = jnp.where(valid, clipped, micro)
        grad = pick(upstream, clipped, rows).astype(single)
        if tick > 0:
            arrived = from_behind(returned, "section", -1)
            grad = grad + arrived.astype(single)
        saved = jax.tree.map(
            lambda buffer: lax.dynamic_index_in_dim(buffer, slot, 0, keepdims=False), store
        )
        d_in, d_memory, d_weights = lax.cond(
            valid, run_backward, skip_backward, grad, saved, meta_at(clipped)
        )
        accum = tuple((total + term for total, term in zip(accum, d_weights)))
        returned = d_in.astype(half)
        given = lax.dynamic_update_slice_in_dim(given, returned, slot * rows, 0)
        memory_grads = lax.dynamic_update_slice_in_dim(
            memory_grads, d_memory.astype(half), slot * frames, 0
        )
    summed = (
        lax.psum_scatter(accum[0][None], "dp", scatter_dimension=1, tiled=True),
        lax.psum_scatter(accum[1][None], "dp", scatter_dimension=1, tiled=True),
        lax.psum_scatter(accum[2][None], "dp", scatter_dimension=1, tiled=True),
        lax.psum_scatter(accum[3][None], "dp", scatter_dimension=1, tiled=True),
        lax.psum_scatter(accum[4][None], "dp", scatter_dimension=1, tiled=True),
        lax.psum_scatter(accum[5][None], "dp", scatter_dimension=1, tiled=True),
        lax.psum_scatter(accum[6][None], "dp", scatter_dimension=1, tiled=True),
        lax.psum_scatter(accum[7][None], "dp", scatter_dimension=2, tiled=True),
        lax.psum_scatter(accum[8][None], "dp", scatter_dimension=2, tiled=True),
    )
    return (
        held[: micro * rows][None],
        given[: micro * rows][None],
        memory_grads[: micro * frames][None],
        summed[0],
        summed[1],
        summed[2],
        summed[3],
        summed[4],
        summed[5],
        summed[6],
        summed[7],
        summed[8],
    )


def solution(mesh):
    in_specs = (
        P("dp", None),
        P("section", "dp", None),
        P("section", "dp", None),
        P("section", "dp", None),
        P("section", "dp", None),
        P("section", "dp", None),
        P("section", "dp", None),
        P("section", "dp", None),
        P("section", None, "dp"),
        P("section", None, "dp"),
        P("section", "dp", None),
        P("dp"),
        P("dp"),
        P("dp", None),
        P("section", "dp", None),
    )
    out_specs = (
        P("section", "dp", None),
        P("section", "dp", None),
        P("section", "dp", None),
        P("section", "dp", None),
        P("section", "dp", None),
        P("section", "dp", None),
        P("section", "dp", None),
        P("section", "dp", None),
        P("section", "dp", None),
        P("section", "dp", None),
        P("section", None, "dp"),
        P("section", None, "dp"),
    )
    return jax.shard_map(
        per_device, mesh=mesh, in_specs=in_specs, out_specs=out_specs, check_vma=False
    )
```

profile of v0, /device:TPU:0, one launch (start us, length us, event | category | flops | bytes accessed | tf_op | source)
XLA Modules:
  0.0 3466.5 jit_solution(14038480969881335312)
XLA Ops:
  19.7 47.0 %all_gather.36 = bf16[1,3,1024]{1,0,2:T(2,128)(2,1)S(1)} all-gather(bf16[1,3,64]{1,0,2:T(2,128)(2,1)S(1)} %copy.380), channel_id=1, replica_groups=mesh['section'=2,'dp'=16] {'dp'}, dimensions={2}, use_global_device_ids=true | all-gather | bytes 6528 | tf_op jit(solution)/shard_map/all_gather | solution.py:283
  67.1 39.5 %all_gather.35 = bf16[1,2,1024]{1,0,2:T(2,128)(2,1)S(1)} all-gather(bf16[1,2,64]{1,0,2:T(2,128)(2,1)S(1)} %copy.377), channel_id=1, replica_groups=mesh['section'=2,'dp'=16] {'dp'}, dimensions={2}, use_global_device_ids=true | all-gather | bytes 4352 | tf_op jit(solution)/shard_map/all_gather | solution.py:284
  111.9 31.4 all-gather.14.cloned.1.call-done
  143.3 62.7 %all-gather.16.cloned.1.call-done = bf16[1,1024,1024]{2,1,0:T(8,128)(2,1)} async-done(((bf16[1,64,1024]{2,1,0:T(8,128)(2,1)}), bf16[1,1024,1024]{2,1,0:T(8,128)(2,1)}) %all-gather.16.cloned.1.call-update) | async-done | bytes 2097168 | tf_op jit(solution)/shard_map/all_gather | solution.py:280
  206.1 78.0 %all-gather.12.cloned.1.call-done = bf16[1,1024,2048]{2,1,0:T(8,128)(2,1)} async-done(((bf16[1,64,2048]{2,1,0:T(8,128)(2,1)}), bf16[1,1024,2048]{2,1,0:T(8,128)(2,1)}) %all-gather.12.cloned.1.call-update) | async-done | bytes 4194320 | tf_op jit(solution)/shard_map/all_gather | solution.py:279
  284.0 96.0 %all-gather.8.cloned.1.call-done = bf16[1,1024,3072]{2,1,0:T(8,128)(2,1)} async-done(((bf16[1,64,3072]{2,1,0:T(8,128)(2,1)}), bf16[1,1024,3072]{2,1,0:T(8,128)(2,1)}) %all-gather.8.cloned.1.call-update) | async-done | bytes 6291472 | tf_op jit(solution)/shard_map/all_gather | solution.py:276
  380.0 114.3 %all-gather.18.cloned.1.call-done = bf16[1,1024,4096]{2,1,0:T(8,128)(2,1)} async-done(((bf16[1,64,4096]{2,1,0:T(8,128)(2,1)}), bf16[1,1024,4096]{2,1,0:T(8,128)(2,1)}) %all-gather.18.cloned.1.call-update) | async-done | bytes 8388624 | tf_op jit(solution)/shard_map/all_gather | solution.py:281
  494.3 114.4 %all-gather.20.cloned.1.call-done = bf16[1,4096,1024]{2,1,0:T(8,128)(2,1)} async-done(((bf16[1,256,1024]{2,1,0:T(8,128)(2,1)}), bf16[1,4096,1024]{2,1,0:T(8,128)(2,1)}) %all-gather.20.cloned.1.call-update) | async-done | bytes 8388624 | tf_op jit(solution)/shard_map/all_gather | solution.py:282
  608.7 133.0 %conditional.6 = (bf16[512,1024]{1,0:T(8,128)(2,1)}, f32[1,512,1024]{2,1,0:T(8,128)}, f32[1,1,16,512]{3,2,1,0:T(8,128)}, f32[1,512,1024]{2,1,0:T(8,128)}, bf16[1...) conditional(s32[]{:T(128)} %convert_element_type.716, ...), branch_computations={%region_0.1_spmd, %region_1.13_spmd} | conditional | flops 19587911680 | bytes 368717312 | solution.py:340
  697.3 32.3 add_convert_fusion
  789.7 141.7 %conditional.7 = (bf16[512,1024]{1,0:T(8,128)(2,1)}, f32[1,512,1024]{2,1,0:T(8,128)}, f32[1,1,16,512]{3,2,1,0:T(8,128)}, f32[1,512,1024]{2,1,0:T(8,128)}, bf16[1...) conditional(s32[]{:T(128)} %convert_element_type.726, ...), branch_computations={%region_12.14_spmd, %region_13.25_spmd} | conditional | flops 19589484544 | bytes 363478432 | solution.py:340
  886.1 32.2 add_convert_fusion.1
  1004.9 42.5 %conditional.9 = (f32[1024,3072]{1,0:T(8,128)}, f32[1024,1024]{1,0:T(8,128)}, f32[1024,1024]{1,0:T(8,128)}, f32[1024,1024]{1,0:T(8,128)}, f32[1024,4096]{1,0:T(8...) conditional(s32[]{:T(128)} %convert_element_type.727, ...), branch_computations={%region_36.38_spmd, %region_37.58_spmd} | conditional | flops 44345319424 | bytes 963966656 | solution.py:392
  1048.7 335.2 %collective-permute-done.2 = bf16[512,1024]{1,0:T(8,128)(2,1)S(1)} collective-permute-done((bf16[512,1024]{1,0:T(8,128)(2,1)}, bf16[512,1024]{1,0:T(8,128)(2,1)S(1)}, u32[]{:S(2)}, u32[]{:S(2)}) %collective-permute-start.2) | collective-permute-done | bytes 1048608 | tf_op jit(solution)/shard_map/ppermute | solution.py:17
  1384.2 262.2 %conditional.10 = (f32[1024,3072]{1,0:T(8,128)}, f32[1024,1024]{1,0:T(8,128)S(1)}, f32[1024,1024]{1,0:T(8,128)S(1)}, f32[1024,1024]{1,0:T(8,128)S(1)}, f32[1024,...) conditional(s32[]{:T(128)} %convert_element_type.726, ...), branch_computations={%region_57.59_spmd, %region_58.79_spmd} | conditional | flops 44337979392 | bytes 1066708800 | solution.py:392
  1397.1 25.5 add_convert_fusion.4
  1656.0 265.8 %conditional.11 = (f32[1024,3072]{1,0:T(8,128)}, f32[1024,1024]{1,0:T(8,128)}, f32[1024,1024]{1,0:T(8,128)}, f32[1024,1024]{1,0:T(8,128)}, f32[1024,4096]{1,0:T(...) conditional(s32[]{:T(128)} %convert_element_type.716, ...), branch_computations={%region_78.80_spmd, %region_79.100_spmd} | conditional | flops 44337979392 | bytes 1033096960 | solution.py:392
  2075.3 92.6 %reduce-scatter.22.cloned.1.call-done = f32[1,64,1024]{2,1,0:T(8,128)} async-done(((f32[1,1024,1024]{2,1,0:T(8,128)}), f32[1,64,1024]{2,1,0:T(8,128)}) %reduce-scatter.22.cloned.1.call-update) | async-done | bytes 262160 | tf_op jit(solution)/shard_map/reduce_scatter | solution.py:406
  2167.9 97.7 %reduce-scatter.18.cloned.1.call-done = f32[1,64,1024]{2,1,0:T(8,128)} async-done(((f32[1,1024,1024]{2,1,0:T(8,128)}), f32[1,64,1024]{2,1,0:T(8,128)}) %reduce-scatter.18.cloned.1.call-update) | async-done | bytes 262160 | tf_op jit(solution)/shard_map/reduce_scatter | solution.py:404
  2265.6 97.5 %reduce-scatter.16.cloned.1.call-done = f32[1,64,1024]{2,1,0:T(8,128)} async-done(((f32[1,1024,1024]{2,1,0:T(8,128)}), f32[1,64,1024]{2,1,0:T(8,128)}) %reduce-scatter.16.cloned.1.call-update) | async-done | bytes 262160 | tf_op jit(solution)/shard_map/reduce_scatter | solution.py:403
  2363.1 180.3 %reduce-scatter.20.cloned.1.call-done = f32[1,64,2048]{2,1,0:T(8,128)} async-done(((f32[1,1024,2048]{2,1,0:T(8,128)}), f32[1,64,2048]{2,1,0:T(8,128)}) %reduce-scatter.20.cloned.1.call-update) | async-done | bytes 524304 | tf_op jit(solution)/shard_map/reduce_scatter | solution.py:405
  2543.4 212.6 %reduce-scatter.14.cloned.1.call-done = f32[1,64,3072]{2,1,0:T(8,128)} async-done(((f32[1,1024,3072]{2,1,0:T(8,128)}), f32[1,64,3072]{2,1,0:T(8,128)}) %reduce-scatter.14.cloned.1.call-update) | async-done | bytes 786448 | tf_op jit(solution)/shard_map/reduce_scatter | solution.py:402
  2756.0 348.8 %reduce-scatter.26.cloned.1.call-done = f32[1,256,1024]{2,1,0:T(8,128)} async-done(((f32[1,4096,1024]{2,1,0:T(8,128)}), f32[1,256,1024]{2,1,0:T(8,128)}) %reduce-scatter.26.cloned.1.call-update) | async-done | bytes 1048592 | tf_op jit(solution)/shard_map/reduce_scatter | solution.py:408
  3104.8 354.9 %reduce-scatter.24.cloned.1.call-done = f32[1,64,4096]{2,1,0:T(8,128)} async-done(((f32[1,1024,4096]{2,1,0:T(8,128)}), f32[1,64,4096]{2,1,0:T(8,128)}) %reduce-scatter.24.cloned.1.call-update) | async-done | bytes 1048592 | tf_op jit(solution)/shard_map/reduce_scatter | solution.py:407
  (741 shorter events, 1061.9 us)
Async XLA Ops:
  7.2 104.7 %all-gather.10.cloned.1.call-start = ((), (), s32[]{:S(2)}) async-start(), calls=%async_computation.10 | async-start | bytes 2228224 | tf_op jit(solution)/shard_map/all_gather | solution.py:277
  9.0 134.3 %all-gather.14.cloned.1.call-start = ((), (), s32[]{:S(2)}) async-start(), calls=%async_computation.12 | async-start | bytes 2228224 | tf_op jit(solution)/shard_map/all_gather | solution.py:278
  10.7 195.4 %all-gather.16.cloned.1.call-start = ((), (), s32[]{:S(2)}) async-start(), calls=%async_computation.13 | async-start | bytes 2228224 | tf_op jit(solution)/shard_map/all_gather | solution.py:280
  12.4 271.6 %all-gather.12.cloned.1.call-start = ((), (), s32[]{:S(2)}) async-start(), calls=%async_computation.11 | async-start | bytes 4456448 | tf_op jit(solution)/shard_map/all_gather | solution.py:279
  14.2 365.8 %all-gather.8.cloned.1.call-start = ((), (), s32[]{:S(2)}) async-start(), calls=%async_computation.9 | async-start | bytes 6684672 | tf_op jit(solution)/shard_map/all_gather | solution.py:276
  16.2 592.5 %copy-start.48 = (bf16[1024,1024]{1,0:T(8,128)(2,1)S(1)}, bf16[1024,1024]{1,0:T(8,128)(2,1)}, u32[]{:S(2)}) copy-start(bf16[1024,1024]{1,0:T(8,128)(2,1)} %param.53) | copy-start | bytes 6291460
  16.3 478.1 %all-gather.18.cloned.1.call-start = ((), (), s32[]{:S(2)}) async-start(), calls=%async_computation.14 | async-start | bytes 8912896 | tf_op jit(solution)/shard_map/all_gather | solution.py:281
  18.5 590.2 %all-gather.20.cloned.1.call-start = ((), (), s32[]{:S(2)}) async-start(), calls=%async_computation.15 | async-start | bytes 8912896 | tf_op jit(solution)/shard_map/all_gather | solution.py:282
  19.5 2032.0 %reduce-scatter.30.cloned.1.call-start = ((), (), s32[]{:S(2)}) async-start(), calls=%async_computation.24 | async-start | bytes 557056
  67.0 541.7 %copy-start.119 = (bf16[1,3,1024]{2,1,0:T(4,128)(2,1)}, bf16[1,3,1024]{2,1,0:T(4,128)(2,1)S(1)}, u32[]{:S(2)}) copy-start(bf16[1,3,1024]{2,1,0:T(4,128)(2,1)S(1)} %copy.381) | copy-start | bytes 18436
  107.0 501.8 %copy-start.124 = (bf16[1,2,1024]{2,1,0:T(2,128)(2,1)}, bf16[1,2,1024]{2,1,0:T(2,128)(2,1)S(1)}, u32[]{:S(2)}) copy-start(bf16[1,2,1024]{2,1,0:T(2,128)(2,1)S(1)} %copy.378) | copy-start | bytes 12292
  108.3 500.5 %copy-start.136 = (s32[1,512]{1,0:T(1,128)}, s32[1,512]{1,0:T(1,128)S(1)}, u32[]{:S(2)}) copy-start(s32[1,512]{1,0:T(1,128)S(1)} %get-tuple-element.2415) | copy-start | bytes 6148
  741.8 47.9 %collective-permute-start = (bf16[512,1024]{1,0:T(8,128)(2,1)}, bf16[512,1024]{1,0:T(8,128)(2,1)}, u32[]{:S(2)}, u32[]{:S(2)}) collective-permute-start(bf16[512,1024]{1,0:T(8,128)(2,1)} %get-tuple-element.1556), channel_id=1, source_target_pairs={{0,16},{1,17},{2,18},{3,19},{4,20},{5,21},{6,22},{7,23},{8,24},{9,... | collective-permute-start | bytes 3145736 | tf_op jit(solution)/shard_map/ppermute | solution.py:17
  931.5 28.3 collective-permute-start.1
  1047.4 336.5 %collective-permute-start.2 = (bf16[512,1024]{1,0:T(8,128)(2,1)}, bf16[512,1024]{1,0:T(8,128)(2,1)S(1)}, u32[]{:S(2)}, u32[]{:S(2)}) collective-permute-start(bf16[512,1024]{1,0:T(8,128)(2,1)} %get-tuple-element.1589), channel_id=1, source_target_pairs={{16,0},{17,1},{18,2},{19,3},{20,4},{21,5},{22,6},{23,7},{24,8},{25... | collective-permute-start | bytes 3145736 | tf_op jit(solution)/shard_map/ppermute | solution.py:17
  1646.4 4.8 collective-permute-start.3
  1923.6 150.2 %reduce-scatter.28.cloned.1.call-start = ((), (), s32[]{:S(2)}) async-start(), calls=%async_computation.23 | async-start | bytes 557056
  1927.3 240.6 %reduce-scatter.22.cloned.1.call-start = ((), (), s32[]{:S(2)}) async-start(), calls=%async_computation.20 | async-start | bytes 4456448 | tf_op jit(solution)/shard_map/reduce_scatter | solution.py:406
  1936.0 329.6 %reduce-scatter.18.cloned.1.call-start = ((), (), s32[]{:S(2)}) async-start(), calls=%async_computation.18 | async-start | bytes 4456448 | tf_op jit(solution)/shard_map/reduce_scatter | solution.py:404
  1944.7 418.4 %reduce-scatter.16.cloned.1.call-start = ((), (), s32[]{:S(2)}) async-start(), calls=%async_computation.17 | async-start | bytes 4456448 | tf_op jit(solution)/shard_map/reduce_scatter | solution.py:403
  1953.4 590.0 %reduce-scatter.20.cloned.1.call-start = ((), (), s32[]{:S(2)}) async-start(), calls=%async_computation.19 | async-start | bytes 8912896 | tf_op jit(solution)/shard_map/reduce_scatter | solution.py:405
  1967.0 789.0 %reduce-scatter.14.cloned.1.call-start = ((), (), s32[]{:S(2)}) async-start(), calls=%async_computation.16 | async-start | bytes 13369344 | tf_op jit(solution)/shard_map/reduce_scatter | solution.py:402
  1986.2 1118.7 %reduce-scatter.26.cloned.1.call-start = ((), (), s32[]{:S(2)}) async-start(), calls=%async_computation.22 | async-start | bytes 17825792 | tf_op jit(solution)/shard_map/reduce_scatter | solution.py:408
  2010.1 1449.6 %reduce-scatter.24.cloned.1.call-start = ((), (), s32[]{:S(2)}) async-start(), calls=%async_computation.21 | async-start | bytes 17825792 | tf_op jit(solution)/shard_map/reduce_scatter | solution.py:407
  (176 other events, 2531.2 us)
Sparse Core Ops, SparseCore 0:
  11.4 67.8 all-gather.9
  82.6 60.6 all-gather.13
  146.7 59.3 all-gather.15
  209.3 74.7 all-gather.11
  287.2 92.7 all-gather.7
  383.2 111.0 all-gather.17
  497.7 111.0 all-gather.19
  1923.7 74.7 reduce-scatter.29
  2000.9 72.8 reduce-scatter.27
  2076.5 91.4 reduce-scatter.21
  2170.8 94.7 reduce-scatter.17
  2268.3 94.7 reduce-scatter.15
  2366.0 177.3 reduce-scatter.19
  2549.5 206.4 reduce-scatter.13
  2758.8 345.9 reduce-scatter.25
  3107.7 352.0 reduce-scatter.23
where the time goes:
time: 3480 us; the launch traced here: 3470 us
  waiting for transfers between devices  2240 us (64%)
  matrix products  537 us (15%)
  local copies, waits for them, and re-layouts  310 us (9%)
  other arithmetic  254 us (7%)
  blocking collectives  86.5 us (2%)
    reduce_scatter x1, waiting for transfers between devices, per_device(): lax.psum_scatter(accum[5][None], 'dp', scatter_dimension=1, tiled=True)  355 us
    reduce_scatter x1, waiting for transfers between devices, per_device(): lax.psum_scatter(accum[6][None], 'dp', scatter_dimension=1, tiled=True)  349 us
    ppermute x4, waiting for transfers between devices, from_behind(): return lax.ppermute(block, axis, route)  338 us
    reduce_scatter x1, waiting for transfers between devices, per_device(): lax.psum_scatter(accum[0][None], 'dp', scatter_dimension=1, tiled=True)  213 us
    reduce_scatter x1, waiting for transfers between devices, per_device(): lax.psum_scatter(accum[3][None], 'dp', scatter_dimension=1, tiled=True)  180 us
    dot_general x14, matrix products, matmul(): return jnp.dot(left, right, preferred_element_type=jnp.float32)  123 us
    all_gather x1, waiting for transfers between devices, per_device(): lax.all_gather(ffn_out.astype(half), 'dp', axis=1, tiled=True)  114 us
    all_gather x1, waiting for transfers between devices, per_device(): lax.all_gather(ffn_in.astype(half), 'dp', axis=1, tiled=True)  114 us
  transfers between devices with their start and end apart: 20, of which 16 were waited for; matrix products, arithmetic and copies ran while one was open for 6% of the time, Pallas kernels for 0%

commit v1 on v0

v1 whole, which is shorter than its diff:
```python
import functools

import jax
import jax.numpy as jnp
from jax import lax
from jax.experimental import pallas as pl
from jax.experimental.pallas import tpu as pltpu
from jax.sharding import PartitionSpec as P

D = 1024
HEADS = 16
SEQ = 512
EPS = 1e-05
NEG = -1e30
MESH = pl.DeviceIdType.MESH
HALF = jnp.bfloat16
FULL = jnp.float32
TILE = 256
ROWS = 64


def grid_of(n):
    deep = 4 if n % 4 == 0 else 1
    rest = n // deep
    wide = max(k for k in range(1, rest + 1) if rest % k == 0 and k * k <= rest)
    return (deep, wide, rest // wide)


class Place:
    def __init__(self, dims):
        self.dims = dims
        self.chip = lax.axis_index("dp")
        self.core = lax.axis_index("section")
        self.other = 1 - self.core
        deep, wide, long = dims
        self.at = (
            self.chip // (wide * long),
            lax.rem(self.chip // long, wide),
            lax.rem(self.chip, long),
        )

    def shifted(self, axis, step):
        where = list(self.at)
        where[axis] = lax.rem(self.at[axis] + step + self.dims[axis], self.dims[axis])
        return where

    def peer(self, axis, step):
        where = self.shifted(axis, step)
        return (self.core, (where[0] * self.dims[1] + where[1]) * self.dims[2] + where[2])

    def twin(self):
        return (self.other, self.chip)

    def greet(self):
        barrier = pltpu.get_barrier_semaphore()
        peers = [self.peer(a, s) for a in range(3) for s in range(1, self.dims[a])]
        peers.append(self.twin())
        for peer in peers:
            pl.semaphore_signal(barrier, inc=1, device_id=peer, device_id_type=MESH)
        pl.semaphore_wait(barrier, len(peers))


def remote(src, dst, send, recv, peer):
    return pltpu.make_async_remote_copy(
        src_ref=src, dst_ref=dst, send_sem=send, recv_sem=recv, device_id=peer, device_id_type=MESH
    )


def local(src, dst, sem):
    return pltpu.make_async_copy(src, dst, sem)


def nt_dot(left, right):
    return lax.dot_general(
        left, right, (((1,), (1,)), ((), ())), preferred_element_type=FULL
    )


def nn_dot(left, right):
    return jnp.dot(left, right, preferred_element_type=FULL)


def tile(i, size=TILE):
    return pl.ds(pl.multiple_of(i * size, size), size)


def loop(count, body):
    def step(i, carry):
        body(i)
        return carry

    lax.fori_loop(0, count, step, 0)


def lane_half(a):
    lane = lax.broadcasted_iota(jnp.int32, (1, 128), 1)
    return jnp.where((lane // 64) == a, 1.0, 0.0).astype(HALF)


def allowed(keys, first, count, causal):
    key = lax.broadcasted_iota(jnp.int32, (keys, TILE), 0)
    ok = key < count
    if causal:
        ok = ok & (key <= first + lax.broadcasted_iota(jnp.int32, (keys, TILE), 1))
    return ok


ORDER_A = (0, 2, 1)
ORDER_B = (0, 1, 2)


def forward_kernel(
    dims,
    meta,
    pack,
    small,
    hidden,
    frames,
    w_all,
    y_out,
    six_out,
    xt_out,
    actt_out,
    dg_out,
    xh_out,
    rstd_out,
    lse_out,
    vec_out,
    ws,
    res,
    xb,
    mem,
    six,
    xt,
    actn,
    actt,
    dg,
    xh,
    hin,
    yb,
    vecs,
    seed_sem,
    swap_send,
    swap_recv,
    hop_send,
    hop_recv,
    twin_send,
    twin_recv,
    vec_send,
    vec_recv,
    vec_swap,
    in_sem,
    frame_sem,
    y_sem,
    w_sem,
    save_sem,
):
    place = Place(dims)
    core, other, at = place.core, place.other, place.at
    place.greet()

    def seed(g):
        return local(
            pack.at[g, pl.ds(2 * core, 2)],
            w_all.at[pl.ds((core * 4 + g) * 4 + 2 * core, 2), at[0], at[1], at[2]],
            seed_sem.at[g],
        )

    def swap(g):
        return remote(
            pack.at[g, pl.ds(2 * other, 2)],
            w_all.at[pl.ds((core * 4 + g) * 4 + 2 * other, 2), at[0], at[1], at[2]],
            swap_send.at[g],
            swap_recv.at[g],
            place.twin(),
        )

    def swapped(layer, g):
        spot = w_all.at[pl.ds((layer * 4 + g) * 4 + 2 * core, 2), at[0], at[1], at[2]]
        return remote(spot, spot, swap_send.at[g], swap_recv.at[g], place.twin())

    own_vec = vecs.at[core, at[0], at[1], at[2]]
    vec_in = local(small, own_vec, in_sem.at[0])
    vec_in.start()
    mine = pl.ds(core * SEQ, SEQ)
    twins = pl.ds(other * SEQ, SEQ)
    hid_in = local(hidden.at[mine], hin, in_sem.at[1])
    hid_in.start()
    mem_in = local(frames.at[mine], mem.at[core], in_sem.at[2])
    mem_in.start()
    for g in range(4):
        seed(g).start()
        swap(g).start()
    mem_swap = remote(
        frames.at[twins], mem.at[core], frame_sem.at[0], frame_sem.at[1], place.twin()
    )
    mem_swap.start()

    orders = [ORDER_A, ORDER_B] * 8

    def block_of(u):
        return (u // 2) * 4 + 2 * core + u % 2

    def part(order, k, shift):
        index = []
        for axis in range(3):
            if axis in order[:k]:
                index.append(slice(None))
            elif axis == order[k]:
                index.append(place.shifted(axis, -shift)[axis])
            else:
                index.append(at[axis])
        return tuple(index)

    def hop(u, k, step):
        here = w_all.at[(block_of(u),) + part(orders[u], k, 0)]
        return remote(
            here,
            here,
            hop_send.at[u, k, step - 1],
            hop_recv.at[u, k, step - 1],
            place.peer(orders[u][k], step),
        )

    def hop_arrival(u, k, step):
        there = w_all.at[(block_of(u),) + part(orders[u], k, step)]
        return remote(
            there, there, hop_send.at[u, k, step - 1], hop_recv.at[u, k, step - 1], place.twin()
        )

    def twin_copy(u, block):
        return remote(
            w_all.at[block], w_all.at[block], twin_send.at[u], twin_recv.at[u], place.twin()
        )

    def vec_hop(k, step):
        here = vecs.at[(core,) + part(ORDER_B, k, 0)]
        return remote(
            here, here, vec_send.at[k, step - 1], vec_recv.at[k, step - 1],
            place.peer(ORDER_B[k], step),
        )

    def vec_arrival(k, step):
        there = vecs.at[(core,) + part(ORDER_B, k, step)]
        return remote(
            there, there, vec_send.at[k, step - 1], vec_recv.at[k, step - 1], place.twin()
        )

    def vec_twin(layer):
        return remote(
            vecs.at[layer], vecs.at[layer], vec_swap.at[0], vec_swap.at[1], place.twin()
        )

    def vec_event(k):
        if k == 0:
            vec_in.wait()
        if 0 < k <= 3:
            for step in range(1, dims[ORDER_B[k - 1]]):
                vec_arrival(k - 1, step).wait_recv()
        if k < 3:
            for step in range(1, dims[ORDER_B[k]]):
                vec_hop(k, step).start()
        elif k == 3:
            vec_twin(core).start()
        else:
            vec_twin(other).wait_recv()

    def event(u, k):
        layer, g = u // 8, (u // 2) % 4
        if k == 0 and u % 2 == 0:

            @pl.when(core == layer)
            def _():
                seed(g).wait()

            @pl.when(core != layer)
            def _():
                swapped(layer, g).wait_recv()

        if 0 < k <= 3:
            for step in range(1, dims[orders[u][k - 1]]):
                hop_arrival(u, k - 1, step).wait_recv()
        if k < 3:
            for step in range(1, dims[orders[u][k]]):
                hop(u, k, step).start()
        elif k == 3:
            twin_copy(u, block_of(u)).start()
        else:
            twin_copy(u, (u // 2) * 4 + 2 * other + u % 2).wait_recv()

    def service(t):
        for k in (4, 3, 2, 1, 0):
            if t == k:
                vec_event(k)
            s = t - k
            if 0 <= s < 8:
                event(2 * s, k)
                event(2 * s + 1, k)

    def save_to(layer, kind, i):
        src, dst, first = {
            "six": (six, six_out, 0),
            "xt": (xt, xt_out, 6),
            "actt": (actt, actt_out, 12),
            "dg": (dg, dg_out, 16),
            "xh": (xh, xh_out, 20),
        }[kind]
        return local(src.at[i], dst.at[layer, i], save_sem.at[first + i])

    saves = (
        [("six", i) for i in range(6)]
        + [("xt", i) for i in range(6)]
        + [("actt", i) for i in range(4)]
        + [("dg", i) for i in range(4)]
        + [("xh", i) for i in range(3)]
    )

    def weight(s, n):
        return ws[s, :, :, :, :, tile(n)].reshape(D, TILE)

    for t in range(4):
        service(t)
    hid_in.wait()
    mem_in.wait()
    remote(
        frames.at[mine], mem.at[other], frame_sem.at[0], frame_sem.at[1], place.twin()
    ).wait_recv()

    count_self = meta[0, core]
    kind = meta[1, core]
    count_cross = meta[2, core]

    def layer_body(l):
        def guard(what, i):
            @pl.when(l > 0)
            def _():
                save_to(l - 1, what, i).wait()

        def save(what, i):
            save_to(l, what, i).start()

        def fetch(g):
            @pl.when(l == 0)
            def _():
                service(g + 4)

            @pl.when(l == 1)
            def _():
                service(g + 8)

            for q in range(4):
                local(w_all.at[(l * 4 + g) * 4 + q], ws.at[q], w_sem.at[q]).start()

        def ready(g, q):
            local(w_all.at[(l * 4 + g) * 4 + q], ws.at[q], w_sem.at[q]).wait()

        def flip(src, i):
            guard("xt", i)

            def step(n):
                xt[i, tile(n), :] = src[:, tile(n)].T

            loop(D // TILE, step)
            save("xt", i)

        def norm(j):
            gain = vec_out[l, pl.ds(j, 1), :]
            guard("xh", j)

            def step(i):
                rows = tile(i, ROWS)
                v = res[rows, :]
                cent = v - jnp.mean(v, -1, keepdims=True)
                rstd = lax.rsqrt(jnp.mean(cent * cent, -1, keepdims=True) + EPS)
                hat = cent * rstd
                xh[j, rows, :] = hat
                rstd_out[l, j, rows, :] = jnp.broadcast_to(rstd, (ROWS, 128))
                xb[rows, :] = (hat * gain).astype(HALF)

            loop(SEQ // ROWS, step)
            save("xh", j)

        def project(src, s, i):
            guard("six", i)

            def step(n):
                six[i, :, tile(n)] = nn_dot(src[...], weight(s, n)).astype(HALF)

            loop(D // TILE, step)
            save("six", i)

        def attend(qi, ki, vi, which, out, count, causal):
            guard("xt", out)

            def pair(hp):
                cols = tile(hp, 128)
                q2 = six[qi, :, cols] * jnp.asarray(0.125, HALF)
                k2 = six[ki, :, cols]
                vt = six[vi, :, cols].T
                for a in range(2):
                    ka = k2 * lane_half(a)
                    for first in range(0, SEQ, TILE):
                        keys = first + TILE if causal else SEQ
                        s = nt_dot(ka[:keys], q2[first : first + TILE])
                        s = jnp.where(allowed(keys, first, count, causal), s, NEG)
                        top = jnp.max(s, 0, keepdims=True)
                        expo = jnp.exp(s - top)
                        total = jnp.sum(expo, 0, keepdims=True)
                        p = (expo * (1.0 / total)).astype(HALF)
                        o = nn_dot(vt[a * 64 : a * 64 + 64, :keys], p)
                        xt[out, pl.ds(hp * 128 + a * 64, 64), pl.ds(first, TILE)] = o.astype(HALF)
                        lse_out[l, which, hp, pl.ds(a, 1), pl.ds(first, TILE)] = top + jnp.log(
                            total
                        )
                xb[:, cols] = xt[out, tile(hp, 128), :].T

            loop(HEADS // 2, pair)
            save("xt", out)

        def add_product(src, s):
            def step(n):
                res[:, tile(n)] += nn_dot(src[...], weight(s, n))

            loop(D // TILE, step)

        fetch(0)

        @pl.when(l == 0)
        def _():
            rank = D // (dims[0] * dims[1] * dims[2])
            vec_out[...] = jnp.zeros(vec_out.shape, FULL)

            def step(j):
                row = lax.broadcasted_iota(jnp.int32, (128, D), 0)
                col = lax.broadcasted_iota(jnp.int32, (128, D), 1)
                spread = jnp.where((col == j * rank + row) & (row < rank), 1.0, 0.0).astype(HALF)
                z = j // (dims[1] * dims[2])
                y = lax.rem(j // dims[2], dims[1])
                x = lax.rem(j, dims[2])
                for m in range(2):
                    vec_out[m] += nn_dot(vecs[m, z, y, x], spread)

            loop(dims[0] * dims[1] * dims[2], step)

        shift = jnp.where(kind == 1, vec_out[l, pl.ds(4, 1), :], vec_out[l, pl.ds(3, 1), :])

        def begin(i):
            rows = tile(i, ROWS)
            came = jnp.where(l == 0, hin[rows, :].astype(FULL), yb[0, rows, :].astype(FULL))
            res[rows, :] = came + shift

        loop(SEQ // ROWS, begin)
        norm(0)
        flip(xb, 0)
        for q in range(3):
            ready(0, q)
            project(xb, q, q)
        attend(0, 1, 2, 0, 1, count_self, True)
        ready(0, 3)
        add_product(xb, 3)
        norm(1)
        flip(xb, 3)
        fetch(1)
        ready(1, 2)
        project(xb, 2, 3)
        flip(mem.at[l], 2)
        ready(1, 0)
        project(mem.at[l], 0, 4)
        ready(1, 1)
        project(mem.at[l], 1, 5)
        attend(3, 4, 5, 1, 4, count_cross, False)
        ready(1, 3)
        add_product(xb, 3)
        norm(2)
        flip(xb, 5)
        fetch(2)
        for q in range(4):
            ready(2, q)
            guard("dg", q)
            guard("actt", q)

            def up(n, q=q):
                u = nn_dot(xb[...], weight(q, n))
                cdf = 0.5 * (1.0 + lax.erf(u * (0.5**0.5)))
                act = (u * cdf).astype(HALF)
                actn[q, :, tile(n)] = act
                actt[q, tile(n), :] = act.T
                bell = jnp.exp(-0.5 * u * u) * 0.3989422804014327
                dg[q, :, tile(n)] = (cdf + u * bell).astype(HALF)

            loop(D // TILE, up)
            save("dg", q)
            save("actt", q)
        fetch(3)
        for q in range(4):
            ready(3, q)

        def down(n):
            total = res[:, tile(n)]
            for q in range(4):
                total += nn_dot(actn[q], weight(q, n))
            yb[l, :, tile(n)] = total.astype(HALF)

        loop(D // TILE, down)

        @pl.when(core == l)
        def _():
            local(yb.at[l], y_out.at[mine], y_sem.at[0]).start()

        @pl.when(core != l)
        def _():
            remote(yb.at[l], y_out.at[mine], y_sem.at[1], y_sem.at[2], place.twin()).start()

    loop(2, layer_body)

    for what, i in saves:
        save_to(1, what, i).wait()
    local(yb.at[core], y_out.at[mine], y_sem.at[0]).wait()
    remote(yb.at[other], y_out.at[mine], y_sem.at[1], y_sem.at[2], place.twin()).wait_send()
    remote(yb.at[core], y_out.at[twins], y_sem.at[1], y_sem.at[2], place.twin()).wait_recv()
    mem_swap.wait_send()
    for g in range(4):
        swap(g).wait_send()
    for k in range(3):
        for step in range(1, dims[ORDER_B[k]]):
            vec_hop(k, step).wait_send()
    vec_twin(core).wait_send()
    for u in range(16):
        for k in range(3):
            for step in range(1, dims[orders[u][k]]):
                hop(u, k, step).wait_send()
        twin_copy(u, block_of(u)).wait_send()


def run_forward(dims, meta, pack, small, hidden, frames):
    rank = D // (dims[0] * dims[1] * dims[2])
    anyw = pl.BlockSpec(memory_space=pl.ANY)
    vmem = pl.BlockSpec(memory_space=pltpu.VMEM)
    hops = max(dims) - 1
    dma = pltpu.SemaphoreType.DMA
    shape = jax.ShapeDtypeStruct
    return pl.pallas_call(
        functools.partial(forward_kernel, dims),
        out_shape=(
            shape((32,) + dims + (rank, D), HALF),
            shape((2 * SEQ, D), HALF),
            shape((2, 6, SEQ, D), HALF),
            shape((2, 6, D, SEQ), HALF),
            shape((2, 4, D, SEQ), HALF),
            shape((2, 4, SEQ, D), HALF),
            shape((2, 3, SEQ, D), FULL),
            shape((2, 3, SEQ, 128), FULL),
            shape((2, 2, HEADS // 2, 2, SEQ), FULL),
            shape((2, 16, D), FULL),
        ),
        in_specs=[pl.BlockSpec(memory_space=pltpu.SMEM)] + [anyw] * 4,
        out_specs=(anyw,) * 7 + (vmem,) * 3,
        scratch_shapes=[
            pltpu.VMEM((4,) + dims + (rank, D), HALF),
            pltpu.VMEM((SEQ, D), FULL),
            pltpu.VMEM((SEQ, D), HALF),
            pltpu.VMEM((2, SEQ, D), HALF),
            pltpu.VMEM((6, SEQ, D), HALF),
            pltpu.VMEM((6, D, SEQ), HALF),
            pltpu.VMEM((4, SEQ, D), HALF),
            pltpu.VMEM((4, D, SEQ), HALF),
            pltpu.VMEM((4, SEQ, D), HALF),
            pltpu.VMEM((3, SEQ, D), FULL),
            pltpu.VMEM((SEQ, D), HALF),
            pltpu.VMEM((2, SEQ, D), HALF),
            pltpu.VMEM((2,) + dims + (16, 128), HALF),
            dma((4,)),
            dma((4,)),
            dma((4,)),
            dma((16, 3, hops)),
            dma((16, 3, hops)),
            dma((16,)),
            dma((16,)),
            dma((3, hops)),
            dma((3, hops)),
            dma((2,)),
            dma((3,)),
            dma((2,)),
            dma((3,)),
            dma((4,)),
            dma((23,)),
        ],
        compiler_params=pltpu.CompilerParams(
            collective_id=0, has_side_effects=True, vmem_limit_bytes=60 * 2**20
        ),
        cost_estimate=pl.CostEstimate(
            flops=40 * 10**9, bytes_accessed=3 * 10**8, transcendentals=10**7
        ),
    )(meta, pack, small, hidden, frames)


def packed(qkv_weight, out_weight, cross_query, cross_kv, cross_out, ffn_in, ffn_out, chips):
    rank = qkv_weight.shape[1]

    def columns(w):
        return jnp.moveaxis(w[0].astype(HALF).reshape(rank, -1, D), 1, 0)

    inner = ffn_in[0].astype(HALF).reshape(rank, chips, 4, rank)
    inner = inner.transpose(2, 0, 1, 3).reshape(4, rank, D)
    outer = ffn_out[0].astype(HALF).reshape(4, rank, D)
    first = jnp.concatenate([columns(qkv_weight), columns(out_weight)], 0)
    second = jnp.concatenate([columns(cross_kv), columns(cross_query), columns(cross_out)], 0)
    return jnp.stack([first, second, inner, outer])


def small_block(norm_gains, type_embed):
    rows = jnp.concatenate([norm_gains[0], type_embed[0]], 0).astype(HALF)
    return jnp.pad(rows, ((0, 16 - rows.shape[0]), (0, 128 - rows.shape[1])))


RS_EVEN = (1, 2, 0)
RS_ODD = (2, 1, 0)
LAGS = (1, 2, 3, 4)
SLOTS = 8
PAIRS = ((12, 8), (13, 9), (14, 10), (15, 11), (4, 5), (7, 6), (3, 0), (1, 2))


def backward_kernel(
    dims,
    meta,
    cot,
    w_all,
    six_in,
    xt_in,
    actt_in,
    dg_in,
    xh_in,
    rstd,
    lse,
    vec,
    dx_out,
    de_out,
    grad_out,
    small_out,
    cot_land,
    land_s,
    land_0,
    land_1,
    land_2,
    stage,
    ws,
    g,
    dx,
    gb,
    qkv,
    work,
    xtb,
    xh,
    tmp_s,
    tmp_0,
    tmp_1,
    tmp_2,
    dxb,
    deb,
    fin,
    sm,
    sm_land,
    w_sem,
    six_sem,
    xt_sem,
    dg_sem,
    xh_sem,
    cot_sem,
    cot_swap,
    s_send,
    s_recv,
    hop_send,
    hop_recv,
    tmp_sem,
    fin_sem,
    fin_send,
    fin_recv,
    out_sem,
    small_send,
    small_recv,
):
    place = Place(dims)
    core, other, at = place.core, place.other, place.at
    rank = D // (dims[0] * dims[1] * dims[2])
    chunk = D // dims[0]
    place.greet()
    mine = pl.ds(core * SEQ, SEQ)
    twins = pl.ds(other * SEQ, SEQ)
    cot_send = remote(cot.at[twins], cot_land, cot_swap.at[0], cot_swap.at[1], place.twin())
    cot_send.start()
    kind = meta[1, core]

    def load_w(slot, layer, b):
        return local(w_all.at[layer * 16 + b], ws.at[slot], w_sem.at[slot])

    def load_six(slot, layer, i):
        return local(six_in.at[layer, i], qkv.at[slot], six_sem.at[slot])

    def load_xt(slot, layer, i):
        return local(xt_in.at[layer, i], xtb.at[slot], xt_sem.at[slot])

    def load_act(slot, layer, q):
        return local(actt_in.at[layer, q], xtb.at[slot], xt_sem.at[slot])

    def load_dg(slot, layer, q):
        return local(dg_in.at[layer, q], work.at[slot], dg_sem.at[slot])

    def load_xh(layer, j):
        return local(xh_in.at[layer, j], xh, xh_sem.at[0])

    def order_of(parity):
        return RS_EVEN if parity == 0 else RS_ODD

    def widest(order):
        return dims[order[1]]

    def region(order, k, step):
        index = []
        for axis in range(3):
            if axis in order[:k]:
                index.append(at[axis])
            elif axis == order[k]:
                index.append(place.shifted(axis, step)[axis])
            else:
                index.append(slice(None))
        return tuple(index)

    def landing(order, k, u, step):
        if k == 0:
            return land_0.at[u, step - 1, :, pl.ds(0, widest(order))]
        if k == 1:
            return land_1.at[u, step - 1]
        return land_2.at[u, step - 1]

    def hop(u, slot, parity, k, step):
        order = order_of(parity)
        return remote(
            stage.at[(slot,) + region(order, k, step)],
            landing(order, k, u, step),
            hop_send.at[u, k, step - 1],
            hop_recv.at[u, k, step - 1],
            place.peer(order[k], step),
        )

    def steps(parity, k):
        return range(1, dims[order_of(parity)[k]])

    def tmp_load(k, u, parity):
        order = order_of(parity)
        if k == 0:
            return [local(land_s.at[u], tmp_s, tmp_sem.at[0, 0])]
        pairs = []
        for step in steps(parity, k - 1):
            if k == 1:
                dst = tmp_0.at[step - 1, :, pl.ds(0, widest(order))]
            elif k == 2:
                dst = tmp_1.at[step - 1]
            else:
                dst = tmp_2.at[step - 1]
            pairs.append(local(landing(order, k - 1, u, step), dst, tmp_sem.at[k, step - 1]))
        return pairs

    def sib_send(u, parity):
        return remote(
            stage.at[SLOTS + parity], land_s.at[u], s_send.at[u], s_recv.at[u], place.twin()
        )

    def own_block(j):
        return jnp.where(core == 0, PAIRS[j][0], PAIRS[j][1])

    def twin_block(j):
        return jnp.where(core == 0, PAIRS[j][1], PAIRS[j][0])

    def fin_local(u, j):
        return local(fin.at[j % 2], grad_out.at[own_block(j)], fin_sem.at[j % 2])

    def fin_remote(u, j):
        return remote(
            fin.at[j % 2], grad_out.at[own_block(j)], fin_send.at[u], fin_recv.at[u], place.twin()
        )

    def fin_wait(u, j, layer):
        @pl.when(core == layer)
        def _():
            fin_local(u, j).wait()

        @pl.when(core != layer)
        def _():
            fin_remote(u, j).wait_send()

    def arrive(k, u, j):
        parity = j % 2
        if k == 0:
            sib_send(u, parity).wait_recv()
        else:
            for step in steps(parity, k - 1):
                hop(u, j, parity, k - 1, step).wait_recv()
        for load in tmp_load(k, u, parity):
            load.start()

    def add_over(slot, parity, k, where, sources):
        order = order_of(parity)
        free = [axis for axis in range(3) if isinstance(where[axis], slice)]
        sizes = [dims[axis] for axis in free]
        total = 1
        for size in sizes:
            total *= size

        def body(i):
            rest = i
            found = {}
            for axis, size in reversed(list(zip(free, sizes))):
                found[axis] = lax.rem(rest, size)
                rest = rest // size
            index = tuple(found[a] if a in found else where[a] for a in range(3))
            spot = (slot,) + index
            value = stage[spot].astype(FULL)
            for source in sources:
                value += source(index).astype(FULL)
            stage[spot] = value.astype(HALF)

        if total == 1:
            body(0)
        else:
            loop(total, body)

    def process(k, u, j, layer):
        parity = j % 2
        order = order_of(parity)
        for load in tmp_load(k, u, parity):
            load.wait()
        if k == 0:
            sources = [lambda index: tmp_s[index]]
        elif k == 1:
            sources = [
                lambda index, step=step: tmp_0[step - 1, index[0], index[order[1]]]
                for step in steps(parity, 0)
            ]
        elif k == 2:
            sources = [
                lambda index, step=step: tmp_1[step - 1, index[0]] for step in steps(parity, 1)
            ]
        if k < 3:
            for step in steps(parity, k):
                add_over(j, parity, k, region(order, k, step), sources)
                hop(u, j, parity, k, step).start()
            add_over(j, parity, k, region(order, k, 0), sources)
        else:

            def free(v, w, its):
                fin_wait(v, w, its)

            if isinstance(u, int):
                if u >= 2:
                    free(u - 2, (j - 2) % 8, 1 - (u - 2) // 8)
            else:

                @pl.when(u >= 2)
                def _():
                    free(u - 2, (j - 2) % 8, 1 - (u - 2) // 8)

            value = stage[(j,) + at].astype(FULL)
            for step in steps(parity, 2):
                value += tmp_2[step - 1].astype(FULL)
            fin[j % 2] = value

            @pl.when(core == layer)
            def _():
                fin_local(u, j).start()

            @pl.when(core != layer)
            def _():
                fin_remote(u, j).start()

            for kk in range(3):
                for step in steps(parity, kk):
                    hop(u, j, parity, kk, step).wait_send()

    def sum_step(it, j):
        todo = []
        for k in range(4):
            back = j - LAGS[k]
            todo.append((k, it * 8 + back, back % 8, back >= 0))

        def guarded(fn):
            for k, u, jj, sure in todo:
                layer = (1 - it) if sure else (2 - it)
                if sure:
                    fn(k, u, jj, layer)
                else:

                    @pl.when(it > 0)
                    def _():
                        fn(k, u, jj, layer)

        guarded(lambda k, u, jj, layer: arrive(k, u, jj))
        guarded(process)

    def flush_step(t):
        todo = [(k, t - LAGS[k]) for k in range(4) if 0 <= t - LAGS[k] < 16]
        for k, u in todo:
            arrive(k, u, u % 8)
        for k, u in todo:
            process(k, u, u % 8, 1 - u // 8)

    def rows_of(slot, n):
        return ws[slot, n].reshape(chunk, D)

    def side(j, which):
        return jnp.where(core == which, j, SLOTS + j % 2)

    def outer(index, left, right):
        def body(n):
            value = nn_dot(left[tile(n, chunk), :], right[...])
            stage[index, n] = value.astype(HALF).reshape(dims[1], dims[2], rank, D)

        loop(dims[0], body)

    def back(dst, terms, fresh, as_half=False):
        def body(n):
            cols = tile(n, chunk)
            total = None
            for left, slot in terms:
                part = nt_dot(left[...], rows_of(slot, n))
                total = part if total is None else total + part
            if not fresh:
                total += dst[:, cols]
            dst[:, cols] = total.astype(HALF) if as_half else total

        loop(dims[0], body)

    def pair_free(it, j):
        if j >= 2:
            sib_send(it * 8 + j - 2, j % 2).wait_send()
        else:

            @pl.when(it > 0)
            def _():
                sib_send(it * 8 + j - 2, j % 2).wait_send()

    def emit(it, j):
        sib_send(it * 8 + j, j % 2).start()
        sum_step(it, j)

    def norm_back(layer, j, last):
        gain = vec[layer, pl.ds(j, 1), :]
        load_xh(layer, j).wait()

        def body(i, carry):
            gains, total = carry
            rows = tile(i, ROWS)
            d = dx[rows, :]
            hat = xh[rows, :]
            dn = d * gain
            first = jnp.mean(dn, -1, keepdims=True)
            second = jnp.mean(dn * hat, -1, keepdims=True)
            out = g[rows, :] + rstd[layer, j, rows, :][:, :1] * (dn - first - hat * second)
            g[rows, :] = out
            gb[rows, :] = out.astype(HALF)
            gains = gains + jnp.sum((d * hat).reshape(ROWS // 8, 8, D), 0)
            if last:
                dxb[layer, rows, :] = out.astype(HALF)
                total = total + jnp.sum(out.reshape(ROWS // 8, 8, D), 0)
            return gains, total

        zero = jnp.zeros((8, D), FULL)
        gains, total = lax.fori_loop(0, SEQ // ROWS, body, (zero, zero))
        sm[0, layer, pl.ds(j, 1), :] = jnp.sum(gains, 0, keepdims=True)
        if last:
            whole = jnp.sum(total, 0, keepdims=True)
            sm[0, layer, pl.ds(3, 1), :] = jnp.where(kind == 1, 0.0, whole)
            sm[0, layer, pl.ds(4, 1), :] = jnp.where(kind == 1, whole, 0.0)

    def attend_back(layer, which, count, causal):
        def pair(hp):
            cols = tile(hp, 128)
            q2 = qkv[0, :, cols] * jnp.asarray(0.125, HALF)
            k2 = qkv[1, :, cols]
            v2 = qkv[2, :, cols]
            do2 = work[3, :, cols]
            kt = k2.T
            dk = [None, None]
            dv = [None, None]
            dq = []

            def put(acc, value, keys):
                for h in range(keys // TILE):
                    piece = value[h * TILE : (h + 1) * TILE]
                    acc[h] = piece if acc[h] is None else acc[h] + piece

            for a in range(2):
                half = lane_half(a)
                ka, va, qa, da = k2 * half, v2 * half, q2 * half, do2 * half
                parts = []
                for first in range(0, SEQ, TILE):
                    span = slice(first, first + TILE)
                    keys = first + TILE if causal else SEQ
                    s = nt_dot(ka[:keys], q2[span])
                    shift = lse[layer, which, hp, pl.ds(a, 1), pl.ds(first, TILE)]
                    p = jnp.where(allowed(keys, first, count, causal), jnp.exp(s - shift), 0.0)
                    dp = nt_dot(va[:keys], do2[span])
                    mix = jnp.sum(dp * p, 0, keepdims=True)
                    ds = (p * (dp - mix)).astype(HALF)
                    put(dv, nn_dot(p.astype(HALF), da[span]), keys)
                    put(dk, nn_dot(ds, qa[span]), keys)
                    parts.append(nn_dot(kt[a * 64 : a * 64 + 64, :keys], ds))
                dq.append(jnp.concatenate(parts, 1))
            whole = jnp.concatenate(dq, 0) * 0.125
            work[0, :, cols] = whole.T.astype(HALF)
            for h in range(SEQ // TILE):
                rows = pl.ds(h * TILE, TILE)
                work[1, rows, cols] = dk[h].astype(HALF)
                work[2, rows, cols] = dv[h].astype(HALF)

        loop(HEADS // 2, pair)

    def give(layer, src, dst, base):
        @pl.when(core == layer)
        def _():
            local(src.at[layer], dst.at[mine], out_sem.at[base]).start()

        @pl.when(core != layer)
        def _():
            remote(
                src.at[layer], dst.at[mine], out_sem.at[base + 1], out_sem.at[base + 2],
                place.twin(),
            ).start()

    def give_done(src, dst, base):
        local(src.at[core], dst.at[mine], out_sem.at[base]).wait()
        remote(
            src.at[other], dst.at[mine], out_sem.at[base + 1], out_sem.at[base + 2], place.twin()
        ).wait_send()
        remote(
            src.at[core], dst.at[twins], out_sem.at[base + 1], out_sem.at[base + 2], place.twin()
        ).wait_recv()

    for slot, b in ((0, 12), (1, 8), (2, 13), (3, 9)):
        load_w(slot, 1, b).start()

    def layer_body(it):
        l = 1 - it
        count_self = meta[0, core]
        count_cross = meta[2, core]

        @pl.when(core == l)
        def _():
            local(cot.at[mine], dxb.at[l], cot_sem.at[0]).start()

        @pl.when(core != l)
        def _():
            remote(
                cot.at[mine], cot_land, cot_swap.at[0], cot_swap.at[1], place.twin()
            ).wait_recv()
            local(cot_land, dxb.at[l], cot_sem.at[0]).start()

        for slot in range(2):
            load_dg(slot, l, slot).start()
        load_xt(0, l, 5).start()
        for q in range(2):
            load_act(1 + q, l, q).start()
        load_xt(3, l, 2).start()
        for i in range(3):
            load_six(i, l, 3 + i).start()
        load_xh(l, 2).start()
        local(cot.at[mine], dxb.at[l], cot_sem.at[0]).wait()

        def begin(i):
            rows = tile(i, ROWS)
            value = dxb[l, rows, :].astype(FULL)
            value = value + jnp.where(it > 0, dxb[1, rows, :].astype(FULL), 0.0)
            g[rows, :] = value
            gb[rows, :] = value.astype(HALF)

        loop(SEQ // ROWS, begin)

        for q in range(4):
            pair = 2 * (q % 2)
            pair_free(it, q)
            load_w(pair, l, 12 + q).wait()
            load_dg(q % 2, l, q).wait()

            def down(n, q=q, pair=pair):
                cols = tile(n, chunk)
                d = nt_dot(gb[...], rows_of(pair, n))
                work[3, :, cols] = (d * work[q % 2, :, cols].astype(FULL)).astype(HALF)

            loop(dims[0], down)
            load_act(1 + q % 2, l, q).wait()
            outer(side(q, 0), xtb.at[1 + q % 2], gb)
            if q == 0:
                load_xt(0, l, 5).wait()
            outer(side(q, 1), xtb.at[0], work.at[3])
            emit_after = q
            load_w(pair + 1, l, 8 + q).wait()
            back(dx, [(work.at[3], pair + 1)], q == 0)
            if q < 2:
                load_w(pair, l, 14 + q).start()
                load_w(pair + 1, l, 10 + q).start()
                load_dg(q, l, q + 2).start()
                load_act(1 + q, l, q + 2).start()
            elif q == 2:
                load_w(0, l, 7).start()
                load_w(1, l, 6).start()
                load_xt(1, l, 4).start()
            else:
                load_w(2, l, 4).start()
                load_w(3, l, 5).start()
                load_xt(2, l, 3).start()
                load_xt(0, l, 1).start()
            emit(it, emit_after)
        norm_back(l, 2, False)
        load_xh(l, 1).start()

        load_w(0, l, 7).wait()
        back(work.at[3], [(gb, 0)], True, True)
        load_w(0, l, 3).start()
        for i in range(3):
            load_six(i, l, 3 + i).wait()
        attend_back(l, 1, count_cross, False)
        for i in range(3):
            load_six(i, l, i).start()
        pair_free(it, 4)
        load_xt(3, l, 2).wait()
        outer(side(4, 0), xtb.at[3], work.at[1])
        outer(side(4, 1), xtb.at[3], work.at[2])
        load_xt(3, l, 0).start()
        emit(it, 4)
        load_w(2, l, 4).wait()
        load_w(3, l, 5).wait()
        back(deb.at[l], [(work.at[1], 2), (work.at[2], 3)], True, True)
        load_w(2, l, 0).start()
        load_w(3, l, 1).start()
        give(l, deb, de_out, 3)
        pair_free(it, 5)
        load_xt(1, l, 4).wait()
        outer(side(5, 0), xtb.at[1], gb)
        load_xt(2, l, 3).wait()
        outer(side(5, 1), xtb.at[2], work.at[0])
        emit(it, 5)
        load_w(1, l, 6).wait()
        back(dx, [(work.at[0], 1)], True)
        load_w(1, l, 2).start()
        norm_back(l, 1, False)
        load_xh(l, 0).start()

        load_w(0, l, 3).wait()
        back(work.at[3], [(gb, 0)], True, True)

        @pl.when(it == 0)
        def _():
            load_w(0, 0, 12).start()

        for i in range(3):
            load_six(i, l, i).wait()
        attend_back(l, 0, count_self, True)
        pair_free(it, 6)
        load_xt(0, l, 1).wait()
        outer(side(6, 0), xtb.at[0], gb)
        load_xt(3, l, 0).wait()
        outer(side(6, 1), xtb.at[3], work.at[0])
        emit(it, 6)
        pair_free(it, 7)
        outer(side(7, 0), xtb.at[3], work.at[1])
        outer(side(7, 1), xtb.at[3], work.at[2])
        emit(it, 7)
        load_w(1, l, 2).wait()
        load_w(2, l, 0).wait()
        load_w(3, l, 1).wait()
        back(dx, [(work.at[0], 2), (work.at[1], 3), (work.at[2], 1)], True)

        @pl.when(it == 0)
        def _():
            load_w(1, 0, 8).start()
            load_w(2, 0, 13).start()
            load_w(3, 0, 9).start()

        norm_back(l, 0, True)
        give(l, dxb, dx_out, 0)

    loop(2, layer_body)

    axes = (2, 1, 0)

    def small_hop(k, step, base):
        return remote(
            sm.at[k + 1],
            sm_land.at[base],
            small_send.at[base],
            small_recv.at[base],
            place.peer(axes[k], step),
        )

    def small_twin():
        return remote(sm.at[0], sm_land.at[0], small_send.at[0], small_recv.at[0], place.twin())

    def bases(k):
        first = 1
        for axis in axes[:k]:
            first += dims[axis] - 1
        return [(step, first + step - 1) for step in range(1, dims[axes[k]])]

    def small_event(k):
        if k == 0:
            small_twin().start()
            return
        if k == 1:
            small_twin().wait_recv()
            sm[1] = sm[0] + sm_land[0]
        else:
            value = sm[k - 1]
            for step, base in bases(k - 2):
                small_hop(k - 2, step, base).wait_recv()
                value += sm_land[base]
            if k == 4:
                small_out[...] = value
                return
            sm[k] = value
        for step, base in bases(k - 1):
            small_hop(k - 1, step, base).start()

    for e in range(max(LAGS)):
        if e < 5:
            small_event(e)
        flush_step(16 + e)
    for e in range(max(LAGS), 5):
        small_event(e)

    small_twin().wait_send()
    for k in range(3):
        for step, base in bases(k):
            small_hop(k, step, base).wait_send()
    cot_send.wait_send()
    for u in (14, 15):
        sib_send(u, u % 2).wait_send()
        fin_wait(u, u % 8, 1 - u // 8)
    for j in range(8):
        unit = (1 - core) * 8 + j
        remote(
            fin.at[j % 2],
            grad_out.at[twin_block(j)],
            fin_send.at[unit],
            fin_recv.at[unit],
            place.twin(),
        ).wait_recv()
    give_done(dxb, dx_out, 0)
    give_done(deb, de_out, 3)


def run_backward(dims, meta, cot, w_all, saved):
    rank = D // (dims[0] * dims[1] * dims[2])
    anyw = pl.BlockSpec(memory_space=pl.ANY)
    vmem = pl.BlockSpec(memory_space=pltpu.VMEM)
    hops = max(dims) - 1
    wide = max(dims[1:])
    smalls = 1 + sum(size - 1 for size in dims)
    dma = pltpu.SemaphoreType.DMA
    shape = jax.ShapeDtypeStruct
    return pl.pallas_call(
        functools.partial(backward_kernel, dims),
        out_shape=(
            shape((2 * SEQ, D), HALF),
            shape((2 * SEQ, D), HALF),
            shape((16, rank, D), FULL),
            shape((2, 8, D), FULL),
            shape((SEQ, D), HALF),
            shape((16,) + dims + (rank, D), HALF),
            shape((16, wide - 1, dims[0], wide, rank, D), HALF),
            shape((16, wide - 1, dims[0], rank, D), HALF),
            shape((16, dims[0] - 1, rank, D), HALF),
        ),
        in_specs=[pl.BlockSpec(memory_space=pltpu.SMEM)] + [anyw] * 7 + [vmem] * 3,
        out_specs=(anyw, anyw, anyw, vmem) + (anyw,) * 5,
        scratch_shapes=[
            pltpu.VMEM((SLOTS + 2,) + dims + (rank, D), HALF),
            pltpu.VMEM((4,) + dims + (rank, D), HALF),
            pltpu.VMEM((SEQ, D), FULL),
            pltpu.VMEM((SEQ, D), FULL),
            pltpu.VMEM((SEQ, D), HALF),
            pltpu.VMEM((3, SEQ, D), HALF),
            pltpu.VMEM((4, SEQ, D), HALF),
            pltpu.VMEM((4, D, SEQ), HALF),
            pltpu.VMEM((SEQ, D), FULL),
            pltpu.VMEM(dims + (rank, D), HALF),
            pltpu.VMEM((wide - 1, dims[0], wide, rank, D), HALF),
            pltpu.VMEM((wide - 1, dims[0], rank, D), HALF),
            pltpu.VMEM((dims[0] - 1, rank, D), HALF),
            pltpu.VMEM((2, SEQ, D), HALF),
            pltpu.VMEM((2, SEQ, D), HALF),
            pltpu.VMEM((2, rank, D), FULL),
            pltpu.VMEM((4, 2, 8, D), FULL),
            pltpu.VMEM((smalls, 2, 8, D), FULL),
            dma((4,)),
            dma((3,)),
            dma((4,)),
            dma((2,)),
            dma((1,)),
            dma((1,)),
            dma((2,)),
            dma((16,)),
            dma((16,)),
            dma((16, 3, hops)),
            dma((16, 3, hops)),
            dma((4, hops)),
            dma((2,)),
            dma((16,)),
            dma((16,)),
            dma((6,)),
            dma((smalls,)),
            dma((smalls,)),
        ],
        compiler_params=pltpu.CompilerParams(
            collective_id=1, has_side_effects=True, vmem_limit_bytes=63 * 2**20
        ),
        cost_estimate=pl.CostEstimate(
            flops=80 * 10**9, bytes_accessed=4 * 10**8, transcendentals=10**7
        ),
    )(meta, cot, w_all, *saved)


def per_device(
    inputs,
    qkv_weight,
    out_weight,
    cross_query,
    cross_kv,
    cross_out,
    ffn_in,
    ffn_out,
    norm_gains,
    type_embed,
    encoder,
    lengths,
    seq_types,
    enc_mask,
    cotangent,
):
    chips = lax.axis_size("dp")
    dims = grid_of(chips)
    rank = D // chips
    pack = packed(
        qkv_weight, out_weight, cross_query, cross_kv, cross_out, ffn_in, ffn_out, chips
    )
    small = small_block(norm_gains, type_embed)
    meta = jnp.stack([lengths, seq_types, jnp.sum(enc_mask, 1)])
    w_all, outs, *saved = run_forward(dims, meta, pack, small, inputs, encoder[0])
    grads = run_backward(dims, meta, cotangent[0], w_all, saved)
    d_in, d_mem, blocks, sums = grads[:4]

    def columns(first, last):
        return jnp.moveaxis(blocks[first:last], 0, 1).reshape(1, rank, -1)

    inner = blocks[8:12].reshape(4, rank, chips, rank).transpose(1, 2, 0, 3)
    own = lax.dynamic_index_in_dim(sums, lax.axis_index("section"), 0, keepdims=False)
    own = lax.dynamic_slice_in_dim(own, lax.axis_index("dp") * rank, rank, 1)
    return (
        outs[None],
        d_in[None],
        d_mem[None],
        columns(0, 3),
        blocks[3:4],
        blocks[6:7],
        columns(4, 6),
        blocks[7:8],
        inner.reshape(1, rank, 4 * D),
        blocks[12:16].reshape(1, 4 * rank, D),
        own[None, :3],
        own[None, 3:5],
    )


def solution(mesh):
    rows = P("section", "dp", None)
    cols = P("section", None, "dp")
    in_specs = (
        (P("dp", None),)
        + (rows,) * 7
        + (cols, cols, rows, P("dp"), P("dp"), P("dp", None), rows)
    )
    out_specs = (rows,) * 10 + (cols, cols)
    return jax.shard_map(
        per_device, mesh=mesh, in_specs=in_specs, out_specs=out_specs, check_vma=False
    )
```

time: 3480 us -> 921 us (0.26)
  waiting for transfers between devices: 2240 us -> 0 us
  Pallas kernels: 0 us -> 872 us
  matrix products: 537 us -> 0 us
  local copies, waits for them, and re-layouts: 310 us -> 28.4 us
  other arithmetic: 254 us -> 8.83 us
  blocking collectives: 86.5 us -> 0 us
    reduce_scatter x7 -> x0, waiting for transfers between devices: 1380 us -> none  [the longest x1 355 us: per_device(): lax.psum_scatter(accum[5][None], 'dp', scatter_dimension=1, tiled=True)]
    pallas_call x0 -> x2, Pallas kernels: none -> 872 us  [the longest x1 530 us: run_backward(): pl.pallas_call(functools.partial(backward_kernel, dims), out_shape=(shape...]
    dot_general x70 -> x0, matrix products: 537 us -> none  [the longest x14 123 us: matmul(): return jnp.dot(left, right, preferred_element_type=jnp.float32)]
    all_gather x7 -> x0, waiting for transfers between devices: 497 us -> none  [the longest x1 114 us: per_device(): lax.all_gather(ffn_out.astype(half), 'dp', axis=1, tiled=True)]
    ppermute x4 -> x0, waiting for transfers between devices: 338 us -> none  [from_behind(): return lax.ppermute(block, axis, route)]
    broadcast_in_dim x10 -> x0, other arithmetic: 112 us -> none  [the longest x1 23.9 us: per_device(): accum[6][None]]
    dynamic_update_slice x39 -> x0, local copies, waits for them, and re-layouts: 88.7 us -> none  [the longest x30 76.7 us: per_device(): lax.dynamic_update_index_in_dim(buffer, value, slot, 0)]
    all_gather x2 -> x0, blocking collectives: 86.5 us -> none  [the longest x1 47 us: per_device(): lax.all_gather(norm_gains.astype(half), 'dp', axis=2, tiled=True)]
  transfers between devices with their start and end apart: 20 -> 0, of which waited for: 16 -> 0; matrix products, arithmetic and copies ran while one was open for 6% -> 0% of each run, Pallas kernels for 0% -> 0%
where the time goes in v1:
time: 921 us; the launch traced here: 911 us
  Pallas kernels  872 us (95%)
  local copies, waits for them, and re-layouts  28.4 us (3%)
    pallas_call x1, Pallas kernels, run_backward(): pl.pallas_call(functools.partial(backward_kernel, dims), out_shape=(shape...  530 us
    pallas_call x1, Pallas kernels, run_forward(): pl.pallas_call(functools.partial(forward_kernel, dims), out_shape=(shape(...  342 us

profile of v1, /device:TPU:0, one launch (start us, length us, event | category | flops | bytes accessed | tf_op | source)
XLA Modules:
  0.0 910.9 jit_solution(15804676869923344087)
XLA Ops:
  0.7 0.9 reduce_sum.9
  1.5 1.3 pad_add_fusion.meta
  2.8 1.3 convert_element_type.58
  4.2 1.1 convert_element_type.57
  6.2 1.0 convert_element_type.51
  8.0 1.0 convert_element_type.55
  9.0 1.0 convert_element_type.54
  10.4 1.6 pad_maximum_fusion.pack
  12.6 342.0 %shard_map.238 = (bf16[32,4,2,2,64,1024]{5,4,3,2,1,0:T(8,128)(2,1)}, bf16[1024,1024]{1,0:T(8,128)(2,1)}, bf16[2,6,512,1024]{3,2,1,0:T(8,128)(2,1)}, bf16[2,6,102...) custom-call(s32[3,2]{1,0:T(4,128)} %pad_add_fusion.meta, ...), custom_call_target="tpu_custom_call" | custom-call | flops 40000000000 | bytes 300000000 | tf_op jit(solution)/shard_map/pallas_call | solution.py:542
  354.6 530.3 %shard_map.239 = (bf16[1024,1024]{1,0:T(8,128)(2,1)}, bf16[1024,1024]{1,0:T(8,128)(2,1)}, f32[16,64,1024]{2,1,0:T(8,128)}, f32[2,8,1024]{2,1,0:T(8,128)}, bf16[5...) custom-call(s32[3,2]{1,0:T(4,128)} %pad_add_fusion.meta, ...), custom_call_target="tpu_custom_call" | custom-call | flops 80000000000 | bytes 400000000 | tf_op jit(solution)/shard_map/pallas_call | solution.py:1259
  884.9 1.2 slice_bitcast_fusion
  886.7 1.5 reshape.64
  888.1 2.0 fusion.8
  890.1 1.1 slice_bitcast_fusion.1
  891.6 1.2 reshape.65
  892.9 2.7 fusion.7
  896.2 2.7 copy.37
  898.8 3.7 reshape.67
  902.5 0.8 constant_dynamic-slice_fusion
  904.4 1.3 copy.52
  905.7 1.0 copy-done.2
  906.8 1.3 copy.53
  908.1 1.0 copy-done.1
  909.1 1.3 copy.54
  (33 shorter events, 5.3 us)
Async XLA Ops:
  0.6 3.5 copy-start.3
  5.3 1.9 copy-start.4
  6.2 3.8 copy-start.5
  10.4 1.6 copy-start.7
  10.4 1.6 copy-start.6
  898.8 5.6 copy-start
  904.4 2.3 copy-start.2
  906.8 2.3 copy-start.1

commit v2 on v1

v2 whole, which is shorter than its diff:
```python
import functools

import jax
import jax.numpy as jnp
from jax import lax
from jax.experimental import pallas as pl
from jax.experimental.pallas import tpu as pltpu
from jax.sharding import PartitionSpec as P

D = 1024
HEADS = 16
SEQ = 512
EPS = 1e-05
NEG = -1e30
MESH = pl.DeviceIdType.MESH
HALF = jnp.bfloat16
FULL = jnp.float32
TILE = 256
ROWS = 128


def grid_of(n):
    deep = 4 if n % 4 == 0 else 1
    rest = n // deep
    wide = max(k for k in range(1, rest + 1) if rest % k == 0 and k * k <= rest)
    return (deep, wide, rest // wide)


class Place:
    def __init__(self, dims):
        self.dims = dims
        self.chip = lax.axis_index("dp")
        self.core = lax.axis_index("section")
        self.other = 1 - self.core
        deep, wide, long = dims
        self.at = (
            self.chip // (wide * long),
            lax.rem(self.chip // long, wide),
            lax.rem(self.chip, long),
        )

    def shifted(self, axis, step):
        where = list(self.at)
        where[axis] = lax.rem(self.at[axis] + step + self.dims[axis], self.dims[axis])
        return where

    def peer(self, axis, step):
        where = self.shifted(axis, step)
        return (self.core, (where[0] * self.dims[1] + where[1]) * self.dims[2] + where[2])

    def twin(self):
        return (self.other, self.chip)

    def greet(self):
        barrier = pltpu.get_barrier_semaphore()
        peers = [self.peer(a, s) for a in range(3) for s in range(1, self.dims[a])]
        peers.append(self.twin())
        for peer in peers:
            pl.semaphore_signal(barrier, inc=1, device_id=peer, device_id_type=MESH)
        pl.semaphore_wait(barrier, len(peers))


def remote(src, dst, send, recv, peer):
    return pltpu.make_async_remote_copy(
        src_ref=src, dst_ref=dst, send_sem=send, recv_sem=recv, device_id=peer, device_id_type=MESH
    )


def local(src, dst, sem):
    return pltpu.make_async_copy(src, dst, sem)


def nt_dot(left, right):
    return lax.dot_general(
        left, right, (((1,), (1,)), ((), ())), preferred_element_type=FULL
    )


def nn_dot(left, right):
    return jnp.dot(left, right, preferred_element_type=FULL)


def tile(i, size=TILE):
    return pl.ds(pl.multiple_of(i * size, size), size)


def loop(count, body):
    def step(i, carry):
        body(i)
        return carry

    lax.fori_loop(0, count, step, 0)


def lane_half(a):
    lane = lax.broadcasted_iota(jnp.int32, (1, 128), 1)
    return jnp.where((lane // 64) == a, 1.0, 0.0).astype(HALF)


def allowed(keys, first, count, causal):
    key = lax.broadcasted_iota(jnp.int32, (keys, TILE), 0)
    ok = key < count
    if causal:
        ok = ok & (key <= first + lax.broadcasted_iota(jnp.int32, (keys, TILE), 1))
    return ok


ORDER_A = (0, 2, 1)
ORDER_B = (0, 1, 2)
ORDER_C = (2, 0, 1)
ORDER_D = (1, 0, 2)
DEEP_SLOTS = 5
MARGIN = 1.0


def deep_sends(k):
    if k == 0:
        return [
            (0, lambda z: z < 3, 1),
            (1, lambda z: z > 0, -1),
            (2, lambda z: z < 2, 2),
            (3, lambda z: z > 1, -2),
        ]
    return [(4, lambda z: z == 2, 1), (4, lambda z: z == 1, -1)]


def stages_of(order):
    found = []
    for axis in order:
        found += [(axis, 0), (axis, 1)] if axis == 0 else [(axis, 0)]
    return found


class Plan:
    UNIT = 2.85
    LATENCY = 2.0

    def __init__(self):
        self.free = {}
        self.time = 0.0
        self.queue = []
        self.count = 0

    def push(self, ready, event):
        self.queue.append((ready, self.count, event))
        self.count += 1

    def occupy(self, loads):
        end = self.time
        for link, load in loads:
            begin = max(self.time, self.free.get(link, 0.0))
            self.free[link] = begin + load
            end = max(end, begin + load)
        return end + self.LATENCY

    def pop(self, before, allowed=lambda event: True):
        ready = [item for item in self.queue if item[0] <= before and allowed(item[2])]
        if not ready:
            return None
        item = min(ready)
        self.queue.remove(item)
        self.time = max(self.time, item[0])
        return item[2]


def stage_loads(order, k, gather):
    stages = stages_of(order)
    axis, part = stages[k]
    size = (4, 2, 2)
    if gather:
        held = 1
        for other in set(a for a, _ in stages[:k]):
            if other != axis:
                held *= size[other]
    else:
        held = 16
        for other in set(a for a, _ in stages[: k + 1]):
            held //= size[other]
    if axis != 0:
        return [(axis, held * Plan.UNIT)]
    far, near = ("middle", "end") if gather else ("end", "middle")
    if part == 0:
        return [(far, 3 * held * Plan.UNIT), (near, 2 * held * Plan.UNIT)]
    return [(near, held * Plan.UNIT)]


FORWARD_CHUNKS = (
    [(4, None), (2, 0), (1.5, 0), (1.5, 0)] + [(2, 0)] * 4 + [(2, 0), (4, None)]
    + [(2.5, 1), (1.5, 1), (1.5, 1)] + [(2, 1)] * 4 + [(2, 1), (3, None)]
    + [(4, 2)] + [(3.5, 2)] * 3 + [(7, 3)]
)
GATHER_ORDERS = (
    ORDER_A, ORDER_B, ORDER_C, ORDER_D, ORDER_A, ORDER_B, ORDER_C, ORDER_D,
    ORDER_A, ORDER_B, ORDER_C, ORDER_D, ORDER_A, ORDER_B, ORDER_C, ORDER_D,
)
GATHER_WINDOW = 3
GATHER_STAGE = 2


def plan_forward():
    plan = Plan()
    after = {}
    for u in range(GATHER_WINDOW):
        plan.push(0.0, (u, 0))
    following = GATHER_WINDOW
    plan.push(0.0, (-1, 0))
    done = set()

    def take(event, out):
        nonlocal following
        u, k = event
        plan.time += 0.4
        done.add(event)
        out.append(event)
        if u < 0:
            if k < 4:
                plan.push(plan.time + 3.0, (u, k + 1))
            return
        if k < 4:
            loads = stage_loads(GATHER_ORDERS[u], k, True)
            plan.push(plan.occupy(loads), (u, k + 1))
        elif k == 4:
            plan.push(plan.occupy([("twin", 4.0)]), (u, 5))
        if k == GATHER_STAGE and following < 16:
            plan.push(plan.time, (following, 0))
            following += 1

    for layer in range(2):
        for i, (length, group) in enumerate(FORWARD_CHUNKS):
            out = []
            while True:
                event = plan.pop(plan.time - MARGIN)
                if event is None:
                    break
                take(event, out)
            need = [(-1, 4)]
            if group is not None:
                first = 2 * (4 * layer + group)
                need += [(first, 5), (first + 1, 5)]
            while not done.issuperset(need):
                take(plan.pop(1e9), out)
            plan.time += length
            after[layer, i] = out
    assert not plan.queue and following == 16
    return after, plan.time


def forward_kernel(
    dims,
    meta,
    pack,
    small,
    hidden,
    frames,
    w_all,
    y_out,
    six_out,
    xt_out,
    actt_out,
    dg_out,
    xh_out,
    rstd_out,
    lse_out,
    vec_out,
    ws,
    res,
    xb,
    mem,
    six,
    xt,
    actn,
    actt,
    dg,
    xh,
    hin,
    yb,
    vecs,
    seed_sem,
    swap_send,
    swap_recv,
    hop_send,
    hop_recv,
    twin_send,
    twin_recv,
    vec_send,
    vec_recv,
    vec_swap,
    in_sem,
    frame_sem,
    y_sem,
    w_sem,
    save_sem,
):
    place = Place(dims)
    core, other, at = place.core, place.other, place.at
    place.greet()

    def seed(g):
        return local(
            pack.at[g, pl.ds(2 * core, 2)],
            w_all.at[pl.ds((core * 4 + g) * 4 + 2 * core, 2), at[0], at[1], at[2]],
            seed_sem.at[g],
        )

    def swap(g):
        return remote(
            pack.at[g, pl.ds(2 * other, 2)],
            w_all.at[pl.ds((core * 4 + g) * 4 + 2 * other, 2), at[0], at[1], at[2]],
            swap_send.at[g],
            swap_recv.at[g],
            place.twin(),
        )

    def swapped(layer, g):
        spot = w_all.at[pl.ds((layer * 4 + g) * 4 + 2 * core, 2), at[0], at[1], at[2]]
        return remote(spot, spot, swap_send.at[g], swap_recv.at[g], place.twin())

    own_vec = vecs.at[core, at[0], at[1], at[2]]
    vec_in = local(small, own_vec, in_sem.at[0])
    vec_in.start()
    mine = pl.ds(core * SEQ, SEQ)
    twins = pl.ds(other * SEQ, SEQ)
    hid_in = local(hidden.at[mine], hin, in_sem.at[1])
    hid_in.start()
    mem_in = local(frames.at[mine], mem.at[core], in_sem.at[2])
    mem_in.start()
    for g in range(4):
        seed(g).start()
        swap(g).start()
    mem_swap = remote(
        frames.at[twins], mem.at[core], frame_sem.at[0], frame_sem.at[1], place.twin()
    )
    mem_swap.start()

    def block_of(u):
        return (u // 2) * 4 + 2 * core + u % 2

    def part(order, k, place_of):
        axis = stages_of(order)[k][0]
        index = []
        for other_axis in range(3):
            if other_axis == axis:
                index.append(place_of)
            elif other_axis in [a for a, _ in stages_of(order)[:k]]:
                index.append(slice(None))
            else:
                index.append(at[other_axis])
        return tuple(index)

    def stage_copies(order, k, base, prefix, send, recv, sending):
        axis, piece = stages_of(order)[k]
        found = []
        if axis != 0:
            for step in range(1, dims[axis]):
                where = place.shifted(axis, 0 if sending else -step)[axis]
                ref = base.at[prefix + part(order, k, where)]
                sems = (send.at[axis, step - 1], recv.at[axis, step - 1])
                found.append((None, remote(ref, ref, *sems, place.peer(axis, step))))
            return found
        if dims[0] == 1:
            return found
        for slot, test, step in deep_sends(piece):
            sems = (send.at[0, slot], recv.at[0, slot])
            if sending:
                from_z = at[0] if piece == 0 else (0 if step > 0 else dims[0] - 1)
                okay = test(at[0])
            else:
                from_z = at[0] - step if piece == 0 else (0 if step > 0 else dims[0] - 1)
                okay = test(at[0] - step) & (at[0] - step >= 0) & (at[0] - step < dims[0])
                from_z = jnp.clip(from_z, 0, dims[0] - 1)
            ref = base.at[prefix + part(order, k, from_z)]
            found.append((okay, remote(ref, ref, *sems, place.peer(0, step))))
        return found

    def each(copies, act):
        for okay, copy in copies:
            if okay is None:
                act(copy)
            else:
                pl.when(okay)(functools.partial(act, copy))

    def hops_of(u, k, sending):
        return stage_copies(
            GATHER_ORDERS[u], k, w_all, (block_of(u),), hop_send.at[u], hop_recv.at[u], sending
        )

    def vec_hops(k, sending):
        return stage_copies(ORDER_B, k, vecs, (core,), vec_send, vec_recv, sending)

    def twin_copy(u, block):
        return remote(
            w_all.at[block], w_all.at[block], twin_send.at[u], twin_recv.at[u], place.twin()
        )

    def vec_twin(layer):
        return remote(
            vecs.at[layer], vecs.at[layer], vec_swap.at[0], vec_swap.at[1], place.twin()
        )

    def event(u, k):
        if u < 0:
            if k == 0:
                vec_in.wait()
            else:
                each(vec_hops(k - 1, False), lambda copy: copy.wait_recv())
            if k < 4:
                each(vec_hops(k, True), lambda copy: copy.start())
            else:
                vec_twin(core).start()
                vec_twin(other).wait_recv()
            return
        layer, g = u // 8, (u // 2) % 4
        if k == 0 and u % 2 == 0:

            @pl.when(core == layer)
            def _():
                seed(g).wait()

            @pl.when(core != layer)
            def _():
                swapped(layer, g).wait_recv()

        if 0 < k <= 4:
            each(hops_of(u, k - 1, False), lambda copy: copy.wait_recv())
        if k < 4:
            each(hops_of(u, k, True), lambda copy: copy.start())
        elif k == 4:
            twin_copy(u, block_of(u)).start()
        else:
            twin_copy(u, (u // 2) * 4 + 2 * other + u % 2).wait_recv()

    events, _ = plan_forward()

    def save_to(layer, kind, i):
        src, dst, first = {
            "six": (six, six_out, 0),
            "xt": (xt, xt_out, 6),
            "actt": (actt, actt_out, 12),
            "dg": (dg, dg_out, 16),
            "xh": (xh, xh_out, 20),
        }[kind]
        return local(src.at[i], dst.at[layer, i], save_sem.at[first + i])

    saves = (
        [("six", i) for i in range(6)]
        + [("xt", i) for i in range(6)]
        + [("actt", i) for i in range(4)]
        + [("dg", i) for i in range(4)]
        + [("xh", i) for i in range(3)]
    )

    def weight(s, cols=slice(None)):
        block = ws[s, :, :, :, :, cols]
        return block.reshape(D, block.shape[-1])

    def early():
        hid_in.wait()
        mem_in.wait()
        remote(
            frames.at[mine], mem.at[other], frame_sem.at[0], frame_sem.at[1], place.twin()
        ).wait_recv()

    count_self = meta[0, core]
    kind = meta[1, core]
    count_cross = meta[2, core]

    def layer_body(l):
        def guard(what, i):
            @pl.when(l > 0)
            def _():
                save_to(l - 1, what, i).wait()

        def save(what, i):
            save_to(l, what, i).start()

        passed = []

        def point():
            i = len(passed)
            passed.append(i)
            for layer in range(2):
                if events[layer, i]:

                    @pl.when(l == layer)
                    def _(layer=layer):
                        for u, k in events[layer, i]:
                            event(u, k)

        def fetch(g):
            for q in range(4):
                local(w_all.at[(l * 4 + g) * 4 + q], ws.at[q], w_sem.at[q]).start()

        def ready(g, q):
            local(w_all.at[(l * 4 + g) * 4 + q], ws.at[q], w_sem.at[q]).wait()

        def flip(src, i):
            guard("xt", i)

            def step(n):
                xt[i, tile(n), :] = src[:, tile(n)].T

            loop(D // TILE, step)
            save("xt", i)

        def norm(j):
            gain = vec_out[l, pl.ds(j, 1), :]
            guard("xh", j)

            def step(i):
                rows = tile(i, ROWS)
                v = res[rows, :]
                cent = v - jnp.mean(v, -1, keepdims=True)
                rstd = lax.rsqrt(jnp.mean(cent * cent, -1, keepdims=True) + EPS)
                hat = cent * rstd
                xh[j, rows, :] = hat
                rstd_out[l, j, rows, :] = jnp.broadcast_to(rstd, (ROWS, 128))
                xb[rows, :] = (hat * gain).astype(HALF)

            loop(SEQ // ROWS, step)
            save("xh", j)

        def project(src, s, i):
            guard("six", i)

            six[i] = nn_dot(src[...], weight(s)).astype(HALF)
            save("six", i)

        def attend(qi, ki, vi, which, out, count, causal):
            guard("xt", out)

            def pair(hp):
                cols = tile(hp, 128)
                q2 = six[qi, :, cols] * jnp.asarray(0.125, HALF)
                k2 = six[ki, :, cols]
                vt = six[vi, :, cols].T
                ka = [k2 * lane_half(a) for a in range(2)]
                for f in range(0, SEQ, TILE):
                    keys = f + TILE if causal else SEQ
                    scores = [nt_dot(ka[a][:keys], q2[f : f + TILE]) for a in range(2)]
                    probs = []
                    for a in range(2):
                        s = jnp.where(allowed(keys, f, count, causal), scores[a], NEG)
                        top = jnp.max(s, 0, keepdims=True)
                        expo = jnp.exp(s - top)
                        total = jnp.sum(expo, 0, keepdims=True)
                        probs.append((expo * (1.0 / total)).astype(HALF))
                        lse_out[l, which, hp, pl.ds(a, 1), pl.ds(f, TILE)] = top + jnp.log(total)
                    for a in range(2):
                        o = nn_dot(vt[a * 64 : a * 64 + 64, :keys], probs[a])
                        xt[out, pl.ds(hp * 128 + a * 64, 64), pl.ds(f, TILE)] = o.astype(HALF)
                xb[:, cols] = xt[out, tile(hp, 128), :].T

            for part_of in range(4):
                if part_of:
                    point()
                loop(HEADS // 8, lambda hp, part_of=part_of: pair(part_of * (HEADS // 8) + hp))
            save("xt", out)

        def add_product(src, s):
            res[...] += nn_dot(src[...], weight(s))

        point()

        @pl.when(l == 0)
        def _():
            early()
            rank = D // (dims[0] * dims[1] * dims[2])
            vec_out[...] = jnp.zeros(vec_out.shape, FULL)

            def step(j):
                row = lax.broadcasted_iota(jnp.int32, (128, D), 0)
                col = lax.broadcasted_iota(jnp.int32, (128, D), 1)
                spread = jnp.where((col == j * rank + row) & (row < rank), 1.0, 0.0).astype(HALF)
                z = j // (dims[1] * dims[2])
                y = lax.rem(j // dims[2], dims[1])
                x = lax.rem(j, dims[2])
                for m in range(2):
                    vec_out[m] += nn_dot(vecs[m, z, y, x], spread)

            loop(dims[0] * dims[1] * dims[2], step)

        shift = jnp.where(kind == 1, vec_out[l, pl.ds(4, 1), :], vec_out[l, pl.ds(3, 1), :])

        def begin(i):
            rows = tile(i, ROWS)
            came = jnp.where(l == 0, hin[rows, :].astype(FULL), yb[0, rows, :].astype(FULL))
            res[rows, :] = came + shift

        loop(SEQ // ROWS, begin)
        norm(0)
        flip(xb, 0)
        point()
        fetch(0)
        for q in range(3):
            if q:
                point()
            ready(0, q)
            project(xb, q, q)
        point()
        attend(0, 1, 2, 0, 1, count_self, True)
        point()
        ready(0, 3)
        add_product(xb, 3)
        point()
        norm(1)
        flip(xb, 3)
        flip(mem.at[l], 2)
        point()
        fetch(1)
        ready(1, 2)
        project(xb, 2, 3)
        point()
        ready(1, 0)
        project(mem.at[l], 0, 4)
        point()
        ready(1, 1)
        project(mem.at[l], 1, 5)
        point()
        attend(3, 4, 5, 1, 4, count_cross, False)
        point()
        ready(1, 3)
        add_product(xb, 3)
        point()
        norm(2)
        flip(xb, 5)
        for q in range(4):
            point()
            if q == 0:
                fetch(2)
            ready(2, q)
            guard("dg", q)
            guard("actt", q)

            for first in range(0, D, 512):
                cols = slice(first, first + 512)
                u = nn_dot(xb[...], weight(q, cols))
                cdf = 0.5 * (1.0 + lax.erf(u * (0.5**0.5)))
                act = (u * cdf).astype(HALF)
                actn[q, :, cols] = act
                actt[q, cols, :] = act.T
                bell = jnp.exp(-0.5 * u * u) * 0.3989422804014327
                dg[q, :, cols] = (cdf + u * bell).astype(HALF)
            save("dg", q)
            save("actt", q)
        point()
        fetch(3)
        for q in range(4):
            ready(3, q)
        assert len(passed) == len(FORWARD_CHUNKS)

        for first in range(0, D, 512):
            cols = slice(first, first + 512)
            total = res[:, cols]
            for q in range(4):
                total += nn_dot(actn[q], weight(q, cols))
            yb[l, :, cols] = total.astype(HALF)

        @pl.when(core == l)
        def _():
            local(yb.at[l], y_out.at[mine], y_sem.at[0]).start()

        @pl.when(core != l)
        def _():
            remote(yb.at[l], y_out.at[mine], y_sem.at[1], y_sem.at[2], place.twin()).start()

    loop(2, layer_body)

    for what, i in saves:
        save_to(1, what, i).wait()
    local(yb.at[core], y_out.at[mine], y_sem.at[0]).wait()
    remote(yb.at[other], y_out.at[mine], y_sem.at[1], y_sem.at[2], place.twin()).wait_send()
    remote(yb.at[core], y_out.at[twins], y_sem.at[1], y_sem.at[2], place.twin()).wait_recv()
    mem_swap.wait_send()
    for g in range(4):
        swap(g).wait_send()
    for k in range(4):
        each(vec_hops(k, True), lambda copy: copy.wait_send())
    vec_twin(core).wait_send()
    for u in range(16):
        for k in range(4):
            each(hops_of(u, k, True), lambda copy: copy.wait_send())
        twin_copy(u, block_of(u)).wait_send()


def run_forward(dims, meta, pack, small, hidden, frames):
    rank = D // (dims[0] * dims[1] * dims[2])
    anyw = pl.BlockSpec(memory_space=pl.ANY)
    vmem = pl.BlockSpec(memory_space=pltpu.VMEM)
    dma = pltpu.SemaphoreType.DMA
    shape = jax.ShapeDtypeStruct
    return pl.pallas_call(
        functools.partial(forward_kernel, dims),
        out_shape=(
            shape((32,) + dims + (rank, D), HALF),
            shape((2 * SEQ, D), HALF),
            shape((2, 6, SEQ, D), HALF),
            shape((2, 6, D, SEQ), HALF),
            shape((2, 4, D, SEQ), HALF),
            shape((2, 4, SEQ, D), HALF),
            shape((2, 3, SEQ, D), FULL),
            shape((2, 3, SEQ, 128), FULL),
            shape((2, 2, HEADS // 2, 2, SEQ), FULL),
            shape((2, 16, D), FULL),
        ),
        in_specs=[pl.BlockSpec(memory_space=pltpu.SMEM), vmem] + [anyw] * 3,
        out_specs=(anyw,) * 7 + (vmem,) * 3,
        scratch_shapes=[
            pltpu.VMEM((4,) + dims + (rank, D), HALF),
            pltpu.VMEM((SEQ, D), FULL),
            pltpu.VMEM((SEQ, D), HALF),
            pltpu.VMEM((2, SEQ, D), HALF),
            pltpu.VMEM((6, SEQ, D), HALF),
            pltpu.VMEM((6, D, SEQ), HALF),
            pltpu.VMEM((4, SEQ, D), HALF),
            pltpu.VMEM((4, D, SEQ), HALF),
            pltpu.VMEM((4, SEQ, D), HALF),
            pltpu.VMEM((3, SEQ, D), FULL),
            pltpu.VMEM((SEQ, D), HALF),
            pltpu.VMEM((2, SEQ, D), HALF),
            pltpu.VMEM((2,) + dims + (16, 128), HALF),
            dma((4,)),
            dma((4,)),
            dma((4,)),
            dma((16, 3, DEEP_SLOTS)),
            dma((16, 3, DEEP_SLOTS)),
            dma((16,)),
            dma((16,)),
            dma((3, DEEP_SLOTS)),
            dma((3, DEEP_SLOTS)),
            dma((2,)),
            dma((3,)),
            dma((2,)),
            dma((3,)),
            dma((4,)),
            dma((23,)),
        ],
        compiler_params=pltpu.CompilerParams(
            collective_id=0, has_side_effects=True, vmem_limit_bytes=60 * 2**20
        ),
        cost_estimate=pl.CostEstimate(
            flops=40 * 10**9, bytes_accessed=3 * 10**8, transcendentals=10**7
        ),
    )(meta, pack, small, hidden, frames)


def packed(qkv_weight, out_weight, cross_query, cross_kv, cross_out, ffn_in, ffn_out, chips):
    rank = qkv_weight.shape[1]

    def columns(w):
        return jnp.moveaxis(w[0].astype(HALF).reshape(rank, -1, D), 1, 0)

    inner = ffn_in[0].astype(HALF).reshape(rank, chips, 4, rank)
    inner = inner.transpose(2, 0, 1, 3).reshape(4, rank, D)
    outer = ffn_out[0].astype(HALF).reshape(4, rank, D)
    first = jnp.concatenate([columns(qkv_weight), columns(out_weight)], 0)
    second = jnp.concatenate([columns(cross_kv), columns(cross_query), columns(cross_out)], 0)
    return jnp.stack([first, second, inner, outer])


def small_block(norm_gains, type_embed):
    rows = jnp.concatenate([norm_gains[0], type_embed[0]], 0).astype(HALF)
    return jnp.pad(rows, ((0, 16 - rows.shape[0]), (0, 128 - rows.shape[1])))


SUM_A = (1, 2, 0)
SUM_B = (2, 1, 0)
SUM_C = (1, 0, 2)
SUM_D = (2, 0, 1)
SUM_ORDERS = (
    SUM_C, SUM_B, SUM_C, SUM_B, SUM_D, SUM_A, SUM_C, SUM_D,
    SUM_D, SUM_A, SUM_C, SUM_C, SUM_D, SUM_B, SUM_C, SUM_B,
)
SLOTS = 7
PAIRS = ((12, 8), (13, 9), (14, 10), (15, 11), (4, 5), (7, 6), (3, 0), (1, 2))


def deep_sums(k):
    if k == 0:
        return [
            (0, lambda z: z < 3, lambda z: z + 1, 1),
            (1, lambda z: z > 0, lambda z: z - 1, -1),
            (2, lambda z: z == 0, lambda z: 2, 2),
            (3, lambda z: z == 3, lambda z: 1, -2),
            (4, lambda z: z == 0, lambda z: 3, 1),
            (4, lambda z: z == 3, lambda z: 0, -1),
        ]
    return [(2, lambda z: z == 1, lambda z: 3, 2), (3, lambda z: z == 2, lambda z: 0, -2)]


BACKWARD_CHUNKS = (
    [(3, None, None)]
    + [
        c
        for q in range(4)
        for c in ((2, None, None), (1.5, q, None), (1.5, None, q), (1.5, None, None))
    ]
    + [(4, None, None)] + [(3.2, None, None)] * 4
    + [(1.5, 4, None), (1.5, None, 4), (3, None, None)]
    + [(1.5, 5, None), (1.5, None, 5), (5, None, None)] + [(2.6, None, None)] * 4
    + [(1.5, 6, None), (1.5, None, 6), (1.5, 7, None), (1.5, None, 7), (6, None, None)]
)


def landing_kind(order, k):
    if k == 0:
        return "s"
    axis, piece = stages_of(order)[k - 1]
    if axis == 0:
        return "z" if piece else "x"
    return "a"


def plan_backward():
    plan = Plan()
    after = {}
    done = set()
    busy = set()

    def allowed(event):
        what, u, k = event
        return what == "p" or landing_kind(SUM_ORDERS[u], k) not in busy

    def take(event, out):
        what, u, k = event
        done.add(event)
        out.append(event)
        if what == "a":
            busy.add(landing_kind(SUM_ORDERS[u], k))
            plan.time += 0.15
            plan.push(plan.time + (1.5 if k == 0 else 0.8), ("p", u, k))
            return
        busy.discard(landing_kind(SUM_ORDERS[u], k))
        plan.time += 1.5 if k == 0 else 0.5
        if k < 4:
            loads = stage_loads(SUM_ORDERS[u], k, False)
            plan.push(plan.occupy(loads), ("a", u, k + 1))

    for it in range(2):
        for i, (length, begun, sent) in enumerate(BACKWARD_CHUNKS):
            out = []
            while True:
                event = plan.pop(plan.time - MARGIN, allowed)
                if event is None:
                    break
                take(event, out)
            last = -1 if begun is None else it * 8 + begun - SLOTS
            if last >= 0:
                while ("p", last, 4) not in done:
                    take(plan.pop(1e9, allowed), out)
            plan.time += length
            if sent is not None:
                plan.push(plan.occupy([("twin", 4.0)]), ("a", it * 8 + sent, 0))
            after[it, i] = out
    rest = []
    while plan.queue:
        take(plan.pop(1e9, allowed), rest)
    return after, rest, plan.time


def backward_kernel(
    dims,
    meta,
    cot,
    w_all,
    six_in,
    xt_in,
    actt_in,
    dg_in,
    xh_in,
    rstd_in,
    lse,
    vec,
    dx_out,
    de_out,
    grad_out,
    small_out,
    cot_land,
    land_s,
    land_a,
    land_b,
    land_z,
    stage,
    ws,
    g,
    dx,
    gb,
    qkv,
    work,
    xtb,
    xh,
    rstd,
    tmp_s,
    tmp_a,
    tmp_z,
    dxb,
    deb,
    fin,
    sm,
    sm_land,
    w_sem,
    six_sem,
    xt_sem,
    dg_sem,
    xh_sem,
    cot_sem,
    cot_swap,
    s_send,
    s_recv,
    hop_send,
    hop_recv,
    tmp_sem,
    fin_sem,
    fin_send,
    fin_recv,
    out_sem,
    small_send,
    small_recv,
):
    place = Place(dims)
    core, other, at = place.core, place.other, place.at
    rank = D // (dims[0] * dims[1] * dims[2])
    place.greet()
    mine = pl.ds(core * SEQ, SEQ)
    twins = pl.ds(other * SEQ, SEQ)
    cot_send = remote(cot.at[twins], cot_land, cot_swap.at[0], cot_swap.at[1], place.twin())
    cot_send.start()
    kind = meta[1, core]

    def load_w(slot, layer, b):
        return local(w_all.at[layer * 16 + b], ws.at[slot], w_sem.at[slot])

    def load_six(slot, layer, i):
        return local(six_in.at[layer, i], qkv.at[slot], six_sem.at[slot])

    def load_xt(slot, layer, i):
        return local(xt_in.at[layer, i], xtb.at[slot], xt_sem.at[slot])

    def load_act(slot, layer, q):
        return local(actt_in.at[layer, q], xtb.at[slot], xt_sem.at[slot])

    def load_dg(slot, layer, q):
        return local(dg_in.at[layer, q], work.at[slot], dg_sem.at[slot])

    def load_xh(layer, j):
        return local(xh_in.at[layer, j], xh, xh_sem.at[0])

    def load_rstd(layer, j):
        return local(rstd_in.at[layer, j], rstd, xh_sem.at[1])

    def region(order, k, value):
        stages = stages_of(order)
        index = []
        for axis in range(3):
            if axis == stages[k][0]:
                index.append(value)
            elif axis in [a for a, _ in stages[:k]]:
                index.append(at[axis])
            else:
                index.append(slice(None))
        return tuple(index)

    def fit(order, k, pool, slot):
        free = [a for a in range(3) if isinstance(region(order, k, 0)[a], slice)]
        if pool is tmp_a and k > 0:
            return slot + ((slice(None),) if free else (0,)) + (0,)
        if pool is land_a or pool is tmp_a:
            return slot + (slice(None), pl.ds(0, dims[free[1]]))
        if pool is land_b:
            return slot + ((slice(None),) if free else (0,))
        return slot + ((pl.ds(0, dims[free[0]]),) if free else (0,))

    def pools(order, k):
        axis = stages_of(order)[k][0]
        if axis == 0:
            return land_z, tmp_z
        return (land_a if k == 0 else land_b), tmp_a

    def sends(u, k):
        order = SUM_ORDERS[u]
        axis, piece = stages_of(order)[k]
        land = pools(order, k)[0]
        found = []
        if axis != 0:
            options = [
                (step - 1, None, place.shifted(axis, step)[axis], step)
                for step in range(1, dims[axis])
            ]
        elif dims[0] == 1:
            options = []
        else:
            options = [
                (slot, test(at[0]), jnp.clip(block(at[0]), 0, dims[0] - 1), step)
                for slot, test, block, step in deep_sums(piece)
            ]
        for slot, okay, value, step in options:
            copy = remote(
                stage.at[(u % SLOTS,) + region(order, k, value)],
                land.at[fit(order, k, land, (u, slot))],
                hop_send.at[u, axis, slot],
                hop_recv.at[u, axis, slot],
                place.peer(axis, step),
            )
            found.append((okay, copy))
        return found

    def came(u, k):
        axis, piece = stages_of(SUM_ORDERS[u])[k - 1]
        if axis != 0:
            return [(step - 1, None) for step in range(1, dims[axis])]
        if dims[0] == 1:
            return []
        if piece == 0:
            return [(4, (at[0] == 1) | (at[0] == 2))]
        return [(0, at[0] >= 1), (1, at[0] <= 2), (2, at[0] >= 2), (3, at[0] <= 1)]

    def when(okay, act):
        if okay is None:
            act()
        else:
            pl.when(okay)(act)

    def arrivals(u, k):
        order = SUM_ORDERS[u]
        axis = stages_of(order)[k - 1][0]
        land, tmp = pools(order, k - 1)
        for slot, okay in came(u, k):
            spot = land.at[fit(order, k - 1, land, (u, slot))]
            wait = functools.partial(
                remote,
                spot,
                spot,
                hop_send.at[u, axis, slot],
                hop_recv.at[u, axis, slot],
                place.twin(),
            )
            load = functools.partial(
                local,
                spot,
                tmp.at[fit(order, k - 1, tmp, (slot,))],
                tmp_sem.at["sabz".index("z" if axis == 0 else ("a" if k == 1 else "b")), slot],
            )
            yield okay, wait, load

    def s_load(u):
        return local(land_s.at[u], tmp_s, tmp_sem.at[0, 0])

    def sib_send(u, parity):
        return remote(
            stage.at[SLOTS + parity], land_s.at[u], s_send.at[u], s_recv.at[u], place.twin()
        )

    def own_block(j):
        return jnp.where(core == 0, PAIRS[j][0], PAIRS[j][1])

    def twin_block(j):
        return jnp.where(core == 0, PAIRS[j][1], PAIRS[j][0])

    def fin_local(u):
        place_of = finals.index(u) % 2
        return local(fin.at[place_of], grad_out.at[own_block(u % 8)], fin_sem.at[place_of])

    def fin_remote(u):
        return remote(
            fin.at[finals.index(u) % 2],
            grad_out.at[own_block(u % 8)],
            fin_send.at[u],
            fin_recv.at[u],
            place.twin(),
        )

    def fin_wait(u):
        layer = 1 - u // 8
        pl.when(core == layer)(lambda: fin_local(u).wait())
        pl.when(core != layer)(lambda: fin_remote(u).wait_send())

    def add_over(slot, where, sources):
        free = [axis for axis in range(3) if isinstance(where[axis], slice)]
        total = 1
        for axis in free:
            total *= dims[axis]

        def body(i):
            found = {}
            for axis in reversed(free):
                found[axis] = lax.rem(i, dims[axis])
                i = i // dims[axis]
            index = tuple(found.get(a, where[a]) for a in range(3))
            spot = (slot,) + index
            if len(sources) == 1 and sources[0][0] is None:
                stage[spot] = stage[spot] + sources[0][1](index)
                return
            value = stage[spot].astype(FULL)
            for okay, source in sources:
                more = source(index).astype(FULL)
                value += more if okay is None else jnp.where(okay, more, 0.0)
            stage[spot] = value.astype(HALF)

        if total == 1:
            body(0)
        else:
            loop(total, body)

    def sources_of(u, k):
        order = SUM_ORDERS[u]
        tmp = pools(order, k - 1)[1]
        axis = stages_of(order)[k - 1][0]
        free = [a for a in range(3) if isinstance(region(order, k - 1, 0)[a], slice)]

        def source(slot):
            def read(index):
                if tmp is tmp_a and k > 1:
                    return tmp[slot, index[free[0]] if free else 0, 0]
                if tmp is tmp_a:
                    return tmp[slot, index[free[0]], index[free[1]]]
                return tmp[slot, index[free[0]] if free else 0]

            return read

        return [(okay, source(slot)) for slot, okay in came(u, k)]

    def sum_event(what, u, k):
        order = SUM_ORDERS[u]
        slot = u % SLOTS
        if what == "a":
            if k == 0:
                sib_send(u, u % 2).wait_recv()
                s_load(u).start()
                return
            for okay, wait, load in arrivals(u, k):

                def act(wait=wait, load=load):
                    wait().wait_recv()
                    load().start()

                when(okay, act)
            return
        if k == 0:
            axis = order[0]
            s_load(u).wait()
            sources = [(None, lambda index: tmp_s[index])]
            for (okay, copy), step in zip(sends(u, 0), range(1, dims[axis])):
                add_over(slot, region(order, 0, place.shifted(axis, step)[axis]), sources)
                copy.start()
            add_over(slot, region(order, 0, at[axis]), sources)
            return
        for okay, _, load in arrivals(u, k):
            when(okay, lambda load=load: load().wait())
        sources = sources_of(u, k)
        axis, piece = stages_of(order)[k - 1]
        if k < 4:
            if axis == 0 and piece == 0:
                if sources:
                    far = jnp.where(at[0] == 1, dims[0] - 1, 0)
                    pl.when(sources[0][0])(
                        lambda: add_over(slot, region(order, k - 1, far), [(None, sources[0][1])])
                    )
            elif sources:
                add_over(slot, region(order, k - 1, at[axis]), sources)
            for okay, copy in sends(u, k):
                when(okay, lambda copy=copy: copy.start())
            return
        turn = finals.index(u)
        if turn >= 2:
            fin_wait(finals[turn - 2])
        value = stage[(slot,) + at].astype(FULL)
        for okay, source in sources:
            more = source(at).astype(FULL)
            value += more if okay is None else jnp.where(okay, more, 0.0)
        fin[turn % 2] = value
        layer = 1 - u // 8
        pl.when(core == layer)(lambda: fin_local(u).start())
        pl.when(core != layer)(lambda: fin_remote(u).start())
        for kk in range(4):
            for okay, copy in sends(u, kk):
                when(okay, lambda copy=copy: copy.wait_send())

    events, rest, _ = plan_backward()
    in_order = [e for key in sorted(events) for e in events[key]] + rest
    finals = [u for what, u, k in in_order if what == "p" and k == 4]

    chunk = D // dims[0]

    def upper(slot, h):
        return ws[slot, h].reshape(chunk, D)

    def side(it, j, which):
        return jnp.where(core == which, lax.rem(it * 8 + j, SLOTS), SLOTS + j % 2)

    def outer(index, left, right):
        for first in range(0, D, TILE):
            cols = slice(first, first + TILE)
            value = nn_dot(left[...], right[:, cols]).astype(HALF)
            stage[index, :, :, :, :, cols] = value.reshape(dims + (rank, TILE))

    def back(dst, terms, fresh, as_half=False):
        for h in range(dims[0]):
            cols = slice(h * chunk, (h + 1) * chunk)
            total = None
            for left, slot in terms:
                part = nt_dot(left[...], upper(slot, h))
                total = part if total is None else total + part
            if not fresh:
                total += dst[:, cols]
            dst[:, cols] = total.astype(HALF) if as_half else total

    def pair_free(it, j):
        if j >= 2:
            sib_send(it * 8 + j - 2, j % 2).wait_send()
        else:

            @pl.when(it > 0)
            def _():
                sib_send(it * 8 + j - 2, j % 2).wait_send()

    def emit(it, j):
        sib_send(it * 8 + j, j % 2).start()

    def norm_back(layer, j, last):
        gain = vec[layer, pl.ds(j, 1), :]
        load_xh(layer, j).wait()
        load_rstd(layer, j).wait()

        def body(i, carry):
            gains, total = carry
            rows = tile(i, ROWS)
            d = dx[rows, :]
            hat = xh[rows, :]
            dn = d * gain
            first = jnp.mean(dn, -1, keepdims=True)
            second = jnp.mean(dn * hat, -1, keepdims=True)
            out = g[rows, :] + rstd[rows, :][:, :1] * (dn - first - hat * second)
            g[rows, :] = out
            gb[rows, :] = out.astype(HALF)
            gains = gains + jnp.sum((d * hat).reshape(ROWS // 8, 8, D), 0)
            if last:
                dxb[rows, :] = out.astype(HALF)
                total = total + jnp.sum(out.reshape(ROWS // 8, 8, D), 0)
            return gains, total

        zero = jnp.zeros((8, D), FULL)
        gains, total = lax.fori_loop(0, SEQ // ROWS, body, (zero, zero))
        sm[0, layer, pl.ds(j, 1), :] = jnp.sum(gains, 0, keepdims=True)
        if last:
            whole = jnp.sum(total, 0, keepdims=True)
            sm[0, layer, pl.ds(3, 1), :] = jnp.where(kind == 1, 0.0, whole)
            sm[0, layer, pl.ds(4, 1), :] = jnp.where(kind == 1, whole, 0.0)

    def attend_back(layer, which, count, causal, point):
        def pair(hp):
            cols = tile(hp, 128)
            q2 = qkv[0, :, cols] * jnp.asarray(0.125, HALF)
            k2 = qkv[1, :, cols]
            v2 = qkv[2, :, cols]
            do2 = work[3, :, cols]
            kt = k2.T
            dk = [None, None]
            dv = [None, None]

            def put(acc, value, keys):
                for h in range(keys // TILE):
                    piece = value[h * TILE : (h + 1) * TILE]
                    acc[h] = piece if acc[h] is None else acc[h] + piece

            halves = [lane_half(0), lane_half(1)]
            ka, va, qa, da = [[m * half for half in halves] for m in (k2, v2, q2, do2)]
            keys = {f: f + TILE if causal else SEQ for f in range(0, SEQ, TILE)}
            rows = [[], []]
            for f in range(0, SEQ, TILE):
                scores, dps, probs, ds = {}, {}, {}, {}
                for a in range(2):
                    scores[a] = nt_dot(ka[a][: keys[f]], q2[f : f + TILE])
                    dps[a] = nt_dot(va[a][: keys[f]], do2[f : f + TILE])
                for a in range(2):
                    shift = lse[layer, which, hp, pl.ds(a, 1), pl.ds(f, TILE)]
                    p = jnp.exp(scores[a] - shift)
                    p = jnp.where(allowed(keys[f], f, count, causal), p, 0.0)
                    mix = jnp.sum(dps[a] * p, 0, keepdims=True)
                    ds[a] = (p * (dps[a] - mix)).astype(HALF)
                    probs[a] = p.astype(HALF)
                for a in range(2):
                    put(dv, nn_dot(probs[a], da[a][f : f + TILE]), keys[f])
                    put(dk, nn_dot(ds[a], qa[a][f : f + TILE]), keys[f])
                    rows[a].append(nn_dot(kt[a * 64 : a * 64 + 64, : keys[f]], ds[a]))
            dq = [jnp.concatenate(r, 1) for r in rows]
            whole = jnp.concatenate(dq, 0) * 0.125
            work[0, :, cols] = whole.T.astype(HALF)
            for h in range(SEQ // TILE):
                rows = pl.ds(h * TILE, TILE)
                work[1, rows, cols] = dk[h].astype(HALF)
                work[2, rows, cols] = dv[h].astype(HALF)

        for part_of in range(4):
            point()
            loop(HEADS // 8, lambda hp, part_of=part_of: pair(part_of * (HEADS // 8) + hp))

    def give(layer, src, dst, base):
        @pl.when(core == layer)
        def _():
            local(src, dst.at[mine], out_sem.at[base]).start()

        @pl.when(core != layer)
        def _():
            remote(
                src, dst.at[mine], out_sem.at[base + 1], out_sem.at[base + 2], place.twin()
            ).start()

    def given(layer, src, dst, base):
        @pl.when(core == layer)
        def _():
            local(src, dst.at[mine], out_sem.at[base]).wait()

        @pl.when(core != layer)
        def _():
            remote(
                src, dst.at[mine], out_sem.at[base + 1], out_sem.at[base + 2], place.twin()
            ).wait_send()

    def give_done(src, dst, base):
        given(0, src, dst, base)
        remote(
            src, dst.at[twins], out_sem.at[base + 1], out_sem.at[base + 2], place.twin()
        ).wait_recv()

    for slot, b in ((0, 12), (1, 8), (2, 13), (3, 9)):
        load_w(slot, 1, b).start()

    def layer_body(it):
        l = 1 - it
        passed = []

        def point():
            i = len(passed)
            passed.append(i)
            for turn in range(2):
                if events[turn, i]:

                    @pl.when(it == turn)
                    def _(turn=turn):
                        for event in events[turn, i]:
                            sum_event(*event)

        point()
        count_self = meta[0, core]
        count_cross = meta[2, core]

        @pl.when(it > 0)
        def _():
            given(1, deb, de_out, 3)

        @pl.when(core == l)
        def _():
            local(cot.at[mine], deb, cot_sem.at[0]).start()

        @pl.when(core != l)
        def _():
            remote(
                cot.at[mine], cot_land, cot_swap.at[0], cot_swap.at[1], place.twin()
            ).wait_recv()
            local(cot_land, deb, cot_sem.at[0]).start()

        for slot in range(2):
            load_dg(slot, l, slot).start()
        load_xt(0, l, 5).start()
        for q in range(2):
            load_act(1 + q, l, q).start()
        load_xt(3, l, 2).start()
        for i in range(3):
            load_six(i, l, 3 + i).start()
        load_xh(l, 2).start()
        load_rstd(l, 2).start()
        local(cot.at[mine], deb, cot_sem.at[0]).wait()

        def begin(i):
            rows = tile(i, ROWS)
            value = deb[rows, :].astype(FULL)
            value = value + jnp.where(it > 0, g[rows, :].astype(HALF).astype(FULL), 0.0)
            g[rows, :] = value
            gb[rows, :] = value.astype(HALF)

        loop(SEQ // ROWS, begin)

        for q in range(4):
            pair = 2 * (q % 2)
            point()
            load_w(pair, l, 12 + q).wait()
            load_dg(q % 2, l, q).wait()

            for h in range(dims[0]):
                cols = slice(h * chunk, (h + 1) * chunk)
                d = nt_dot(gb[...], upper(pair, h))
                work[3, :, cols] = (d * work[q % 2, :, cols].astype(FULL)).astype(HALF)
            load_act(1 + q % 2, l, q).wait()
            point()
            pair_free(it, q)
            outer(side(it, q, 0), xtb.at[1 + q % 2], gb)
            point()
            if q == 0:
                load_xt(0, l, 5).wait()
            outer(side(it, q, 1), xtb.at[0], work.at[3])
            emit(it, q)
            point()
            load_w(pair + 1, l, 8 + q).wait()
            back(dx, [(work.at[3], pair + 1)], q == 0)
            if q < 2:
                load_w(pair, l, 14 + q).start()
                load_w(pair + 1, l, 10 + q).start()
                load_dg(q, l, q + 2).start()
                load_act(1 + q, l, q + 2).start()
            elif q == 2:
                load_w(0, l, 7).start()
                load_w(1, l, 6).start()
                load_xt(1, l, 4).start()
            else:
                load_w(2, l, 4).start()
                load_w(3, l, 5).start()
                load_xt(2, l, 3).start()
                load_xt(0, l, 1).start()
        point()
        norm_back(l, 2, False)
        load_xh(l, 1).start()
        load_rstd(l, 1).start()

        load_w(0, l, 7).wait()
        back(work.at[3], [(gb, 0)], True, True)
        load_w(0, l, 3).start()
        for i in range(3):
            load_six(i, l, 3 + i).wait()
        attend_back(l, 1, count_cross, False, point)
        for i in range(3):
            load_six(i, l, i).start()
        point()
        pair_free(it, 4)
        load_xt(3, l, 2).wait()
        outer(side(it, 4, 0), xtb.at[3], work.at[1])
        point()
        outer(side(it, 4, 1), xtb.at[3], work.at[2])
        load_xt(3, l, 0).start()
        emit(it, 4)
        point()
        load_w(2, l, 4).wait()
        load_w(3, l, 5).wait()
        back(deb, [(work.at[1], 2), (work.at[2], 3)], True, True)
        load_w(2, l, 0).start()
        load_w(3, l, 1).start()
        give(l, deb, de_out, 3)
        point()
        pair_free(it, 5)
        load_xt(1, l, 4).wait()
        outer(side(it, 5, 0), xtb.at[1], gb)
        point()
        load_xt(2, l, 3).wait()
        outer(side(it, 5, 1), xtb.at[2], work.at[0])
        emit(it, 5)
        point()
        load_w(1, l, 6).wait()
        back(dx, [(work.at[0], 1)], True)
        load_w(1, l, 2).start()
        norm_back(l, 1, False)
        load_xh(l, 0).start()
        load_rstd(l, 0).start()

        load_w(0, l, 3).wait()
        back(work.at[3], [(gb, 0)], True, True)

        @pl.when(it == 0)
        def _():
            load_w(0, 0, 12).start()

        for i in range(3):
            load_six(i, l, i).wait()
        attend_back(l, 0, count_self, True, point)
        point()
        pair_free(it, 6)
        load_xt(0, l, 1).wait()
        outer(side(it, 6, 0), xtb.at[0], gb)
        point()
        load_xt(3, l, 0).wait()
        outer(side(it, 6, 1), xtb.at[3], work.at[0])
        emit(it, 6)
        point()
        pair_free(it, 7)
        outer(side(it, 7, 0), xtb.at[3], work.at[1])
        point()
        outer(side(it, 7, 1), xtb.at[3], work.at[2])
        emit(it, 7)
        point()
        load_w(1, l, 2).wait()
        load_w(2, l, 0).wait()
        load_w(3, l, 1).wait()
        back(dx, [(work.at[0], 2), (work.at[1], 3), (work.at[2], 1)], True)

        @pl.when(it == 0)
        def _():
            load_w(1, 0, 8).start()
            load_w(2, 0, 13).start()
            load_w(3, 0, 9).start()

        @pl.when(it > 0)
        def _():
            given(1, dxb, dx_out, 0)

        norm_back(l, 0, True)
        give(l, dxb, dx_out, 0)
        assert len(passed) == len(BACKWARD_CHUNKS)

    tmp_z[...] = jnp.zeros(tmp_z.shape, HALF)
    loop(2, layer_body)

    axes = (2, 1, 0)

    def small_hop(k, step, base):
        return remote(
            sm.at[k + 1],
            sm_land.at[base],
            small_send.at[base],
            small_recv.at[base],
            place.peer(axes[k], step),
        )

    def small_twin():
        return remote(sm.at[0], sm_land.at[0], small_send.at[0], small_recv.at[0], place.twin())

    def bases(k):
        first = 1
        for axis in axes[:k]:
            first += dims[axis] - 1
        return [(step, first + step - 1) for step in range(1, dims[axes[k]])]

    def small_event(k):
        if k == 0:
            small_twin().start()
            return
        if k == 1:
            small_twin().wait_recv()
            sm[1] = sm[0] + sm_land[0]
        else:
            value = sm[k - 1]
            for step, base in bases(k - 2):
                small_hop(k - 2, step, base).wait_recv()
                value += sm_land[base]
            if k == 4:
                small_out[...] = value
                return
            sm[k] = value
        for step, base in bases(k - 1):
            small_hop(k - 1, step, base).start()

    every = max(1, len(rest) // 5)
    for e in range(5):
        small_event(e)
        for event in rest[e * every : (e + 1) * every if e < 4 else None]:
            sum_event(*event)

    small_twin().wait_send()
    for k in range(3):
        for step, base in bases(k):
            small_hop(k, step, base).wait_send()
    cot_send.wait_send()
    for u in (14, 15):
        sib_send(u, u % 2).wait_send()
    for u in finals[-2:]:
        fin_wait(u)
    for j in range(8):
        unit = (1 - core) * 8 + j
        remote(
            fin.at[j % 2],
            grad_out.at[twin_block(j)],
            fin_send.at[unit],
            fin_recv.at[unit],
            place.twin(),
        ).wait_recv()
    give_done(dxb, dx_out, 0)
    give_done(deb, de_out, 3)


def run_backward(dims, meta, cot, w_all, saved):
    rank = D // (dims[0] * dims[1] * dims[2])
    anyw = pl.BlockSpec(memory_space=pl.ANY)
    vmem = pl.BlockSpec(memory_space=pltpu.VMEM)
    wide = max(dims[1:])
    smalls = 1 + sum(size - 1 for size in dims)
    dma = pltpu.SemaphoreType.DMA
    shape = jax.ShapeDtypeStruct
    return pl.pallas_call(
        functools.partial(backward_kernel, dims),
        out_shape=(
            shape((2 * SEQ, D), HALF),
            shape((2 * SEQ, D), HALF),
            shape((16, rank, D), FULL),
            shape((2, 8, D), FULL),
            shape((SEQ, D), HALF),
            shape((16,) + dims + (rank, D), HALF),
            shape((16, wide - 1, dims[0], wide, rank, D), HALF),
            shape((16, wide - 1, dims[0], rank, D), HALF),
            shape((16, DEEP_SLOTS, wide, rank, D), HALF),
        ),
        in_specs=[pl.BlockSpec(memory_space=pltpu.SMEM)] + [anyw] * 8 + [vmem] * 2,
        out_specs=(anyw, anyw, anyw, vmem) + (anyw,) * 5,
        scratch_shapes=[
            pltpu.VMEM((SLOTS + 2,) + dims + (rank, D), HALF),
            pltpu.VMEM((4,) + dims + (rank, D), HALF),
            pltpu.VMEM((SEQ, D), FULL),
            pltpu.VMEM((SEQ, D), FULL),
            pltpu.VMEM((SEQ, D), HALF),
            pltpu.VMEM((3, SEQ, D), HALF),
            pltpu.VMEM((4, SEQ, D), HALF),
            pltpu.VMEM((4, D, SEQ), HALF),
            pltpu.VMEM((SEQ, D), FULL),
            pltpu.VMEM((SEQ, 128), FULL),
            pltpu.VMEM(dims + (rank, D), HALF),
            pltpu.VMEM((wide - 1, dims[0], wide, rank, D), HALF),
            pltpu.VMEM((DEEP_SLOTS, wide, rank, D), HALF),
            pltpu.VMEM((SEQ, D), HALF),
            pltpu.VMEM((SEQ, D), HALF),
            pltpu.VMEM((2, rank, D), FULL),
            pltpu.VMEM((4, 2, 8, D), FULL),
            pltpu.VMEM((smalls, 2, 8, D), FULL),
            dma((4,)),
            dma((3,)),
            dma((4,)),
            dma((2,)),
            dma((2,)),
            dma((1,)),
            dma((2,)),
            dma((16,)),
            dma((16,)),
            dma((16, 3, DEEP_SLOTS)),
            dma((16, 3, DEEP_SLOTS)),
            dma((4, DEEP_SLOTS)),
            dma((2,)),
            dma((16,)),
            dma((16,)),
            dma((6,)),
            dma((smalls,)),
            dma((smalls,)),
        ],
        compiler_params=pltpu.CompilerParams(
            collective_id=1, has_side_effects=True, vmem_limit_bytes=62 * 2**20
        ),
        cost_estimate=pl.CostEstimate(
            flops=80 * 10**9, bytes_accessed=4 * 10**8, transcendentals=10**7
        ),
    )(meta, cot, w_all, *saved)


def per_device(
    inputs,
    qkv_weight,
    out_weight,
    cross_query,
    cross_kv,
    cross_out,
    ffn_in,
    ffn_out,
    norm_gains,
    type_embed,
    encoder,
    lengths,
    seq_types,
    enc_mask,
    cotangent,
):
    chips = lax.axis_size("dp")
    dims = grid_of(chips)
    rank = D // chips
    pack = packed(
        qkv_weight, out_weight, cross_query, cross_kv, cross_out, ffn_in, ffn_out, chips
    )
    small = small_block(norm_gains, type_embed)
    meta = jnp.stack([lengths, seq_types, jnp.sum(enc_mask, 1)])
    w_all, outs, *saved = run_forward(dims, meta, pack, small, inputs, encoder[0])
    grads = run_backward(dims, meta, cotangent[0], w_all, saved)
    d_in, d_mem, blocks, sums = grads[:4]

    def columns(first, last):
        return jnp.moveaxis(blocks[first:last], 0, 1).reshape(1, rank, -1)

    inner = blocks[8:12].reshape(4, rank, chips, rank).transpose(1, 2, 0, 3)
    own = lax.dynamic_index_in_dim(sums, lax.axis_index("section"), 0, keepdims=False)
    own = lax.dynamic_slice_in_dim(own, lax.axis_index("dp") * rank, rank, 1)
    return (
        outs[None],
        d_in[None],
        d_mem[None],
        columns(0, 3),
        blocks[3:4],
        blocks[6:7],
        columns(4, 6),
        blocks[7:8],
        inner.reshape(1, rank, 4 * D),
        blocks[12:16].reshape(1, 4 * rank, D),
        own[None, :3],
        own[None, 3:5],
    )


def solution(mesh):
    rows = P("section", "dp", None)
    cols = P("section", None, "dp")
    in_specs = (
        (P("dp", None),)
        + (rows,) * 7
        + (cols, cols, rows, P("dp"), P("dp"), P("dp", None), rows)
    )
    out_specs = (rows,) * 10 + (cols, cols)
    return jax.shard_map(
        per_device, mesh=mesh, in_specs=in_specs, out_specs=out_specs, check_vma=False
    )
```

time: 921 us -> 682 us (0.74)
  Pallas kernels: 872 us -> 640 us
    pallas_call x1, Pallas kernels: 530 us -> 318 us  [run_backward(): pl.pallas_call(functools.partial(backward_kernel, dims), out_shape=(shape...]
    pallas_call x1, Pallas kernels: 342 us -> 321 us  [run_forward(): pl.pallas_call(functools.partial(forward_kernel, dims), out_shape=(shape(...]
where the time goes in v2:
time: 682 us; the launch traced here: 678 us
  Pallas kernels  640 us (94%)
  local copies, waits for them, and re-layouts  28.4 us (4%)
  other arithmetic  8.83 us (1%)
    pallas_call x1, Pallas kernels, run_forward(): pl.pallas_call(functools.partial(forward_kernel, dims), out_shape=(shape(...  321 us
    pallas_call x1, Pallas kernels, run_backward(): pl.pallas_call(functools.partial(backward_kernel, dims), out_shape=(shape...  318 us

profile of v2, /device:TPU:0, one launch (start us, length us, event | category | flops | bytes accessed | tf_op | source)
XLA Modules:
  0.0 677.9 jit_solution(16543257646489524567)
XLA Ops:
  0.7 0.9 reduce_sum.9
  1.5 1.3 pad_add_fusion.meta
  2.8 1.3 convert_element_type.58
  4.2 1.1 convert_element_type.57
  6.2 1.0 convert_element_type.51
  8.0 1.0 convert_element_type.55
  9.0 1.0 convert_element_type.54
  10.4 1.6 pad_maximum_fusion.pack
  12.6 321.2 %shard_map.238 = (bf16[32,4,2,2,64,1024]{5,4,3,2,1,0:T(8,128)(2,1)}, bf16[1024,1024]{1,0:T(8,128)(2,1)}, bf16[2,6,512,1024]{3,2,1,0:T(8,128)(2,1)}, bf16[2,6,102...) custom-call(s32[3,2]{1,0:T(4,128)} %pad_add_fusion.meta, ...), custom_call_target="tpu_custom_call" | custom-call | flops 40000000000 | bytes 300000000 | tf_op jit(solution)/shard_map/pallas_call | solution.py:691
  333.8 318.4 %shard_map.239 = (bf16[1024,1024]{1,0:T(8,128)(2,1)}, bf16[1024,1024]{1,0:T(8,128)(2,1)}, f32[16,64,1024]{2,1,0:T(8,128)}, f32[2,8,1024]{2,1,0:T(8,128)}, bf16[5...) custom-call(s32[3,2]{1,0:T(4,128)} %pad_add_fusion.meta, ...), custom_call_target="tpu_custom_call" | custom-call | flops 80000000000 | bytes 400000000 | tf_op jit(solution)/shard_map/pallas_call | solution.py:1584
  652.2 1.2 slice_bitcast_fusion
  653.9 1.5 reshape.64
  655.4 2.0 fusion.8
  657.4 1.1 slice_bitcast_fusion.1
  658.9 1.2 reshape.65
  660.2 2.7 fusion.7
  663.4 2.7 copy.37
  666.1 3.7 reshape.67
  669.8 0.8 constant_dynamic-slice_fusion
  671.7 1.3 copy.52
  673.0 1.0 copy-done.2
  674.0 1.3 copy.53
  675.4 1.0 copy-done.1
  676.4 1.3 copy.54
  (33 shorter events, 5.3 us)
Async XLA Ops:
  0.6 3.5 copy-start.3
  5.3 1.9 copy-start.4
  6.2 3.8 copy-start.5
  10.4 1.6 copy-start.7
  10.4 1.6 copy-start.6
  666.1 5.6 copy-start
  671.7 2.3 copy-start.2
  674.0 2.3 copy-start.1

commit v3 on v2

--- a/solution.py
+++ b/solution.py
@@ -110,7 +110,8 @@
 ORDER_C = (2, 0, 1)
 ORDER_D = (1, 0, 2)
 DEEP_SLOTS = 5
-MARGIN = 1.0
+GATHER_MARGIN = 3.0
+SUM_MARGIN = 0.0
 
 
 def deep_sends(k):
@@ -229,7 +230,7 @@
         for i, (length, group) in enumerate(FORWARD_CHUNKS):
             out = []
             while True:
-                event = plan.pop(plan.time - MARGIN)
+                event = plan.pop(plan.time - GATHER_MARGIN)
                 if event is None:
                     break
                 take(event, out)
@@ -767,8 +768,8 @@
 SUM_C = (1, 0, 2)
 SUM_D = (2, 0, 1)
 SUM_ORDERS = (
-    SUM_C, SUM_B, SUM_C, SUM_B, SUM_D, SUM_A, SUM_C, SUM_D,
-    SUM_D, SUM_A, SUM_C, SUM_C, SUM_D, SUM_B, SUM_C, SUM_B,
+    SUM_C, SUM_B, SUM_C, SUM_B, SUM_D, SUM_A, SUM_C, SUM_B,
+    SUM_D, SUM_B, SUM_C, SUM_C, SUM_B, SUM_D, SUM_C, SUM_B,
 )
 SLOTS = 7
 PAIRS = ((12, 8), (13, 9), (14, 10), (15, 11), (4, 5), (7, 6), (3, 0), (1, 2))
@@ -839,7 +840,7 @@
         for i, (length, begun, sent) in enumerate(BACKWARD_CHUNKS):
             out = []
             while True:
-                event = plan.pop(plan.time - MARGIN, allowed)
+                event = plan.pop(plan.time - SUM_MARGIN, allowed)
                 if event is None:
                     break
                 take(event, out)
@@ -872,7 +873,13 @@
     vec,
     dx_out,
     de_out,
-    grad_out,
+    qkv_grad,
+    out_grad,
+    kv_grad,
+    cq_grad,
+    co_grad,
+    inner_grad,
+    outer_grad,
     small_out,
     cot_land,
     land_s,
@@ -1049,29 +1056,36 @@
             stage.at[SLOTS + parity], land_s.at[u], s_send.at[u], s_recv.at[u], place.twin()
         )
 
-    def own_block(j):
-        return jnp.where(core == 0, PAIRS[j][0], PAIRS[j][1])
-
-    def twin_block(j):
-        return jnp.where(core == 0, PAIRS[j][1], PAIRS[j][0])
-
-    def fin_local(u):
-        place_of = finals.index(u) % 2
-        return local(fin.at[place_of], grad_out.at[own_block(u % 8)], fin_sem.at[place_of])
-
-    def fin_remote(u):
+    def target(b):
+        if b < 3:
+            return qkv_grad.at[:, pl.ds(b * D, D)]
+        if b < 6:
+            return out_grad if b == 3 else kv_grad.at[:, pl.ds((b - 4) * D, D)]
+        if b < 8:
+            return cq_grad if b == 6 else co_grad
+        if b < 12:
+            return inner_grad.at[b - 8]
+        return outer_grad.at[pl.ds((b - 12) * rank, rank)]
+
+    def fin_local(u, side):
+        turn = finals.index(u) % 2
+        return local(fin.at[turn], target(PAIRS[u % 8][side]), fin_sem.at[turn])
+
+    def fin_remote(u, side):
+        turn = finals.index(u) % 2
         return remote(
-            fin.at[finals.index(u) % 2],
-            grad_out.at[own_block(u % 8)],
-            fin_send.at[u],
-            fin_recv.at[u],
-            place.twin(),
+            fin.at[turn], target(PAIRS[u % 8][side]), fin_send.at[u], fin_recv.at[u], place.twin()
         )
+
+    def fin_start(u):
+        layer = 1 - u // 8
+        pl.when(core == layer)(lambda: fin_local(u, layer).start())
+        pl.when(core != layer)(lambda: fin_remote(u, 1 - layer).start())
 
     def fin_wait(u):
         layer = 1 - u // 8
-        pl.when(core == layer)(lambda: fin_local(u).wait())
-        pl.when(core != layer)(lambda: fin_remote(u).wait_send())
+        pl.when(core == layer)(lambda: fin_local(u, layer).wait())
+        pl.when(core != layer)(lambda: fin_remote(u, 1 - layer).wait_send())
 
     def add_over(slot, where, sources):
         free = [axis for axis in range(3) if isinstance(where[axis], slice)]
@@ -1167,9 +1181,7 @@
             more = source(at).astype(FULL)
             value += more if okay is None else jnp.where(okay, more, 0.0)
         fin[turn % 2] = value
-        layer = 1 - u // 8
-        pl.when(core == layer)(lambda: fin_local(u).start())
-        pl.when(core != layer)(lambda: fin_remote(u).start())
+        fin_start(u)
         for kk in range(4):
             for okay, copy in sends(u, kk):
                 when(okay, lambda copy=copy: copy.wait_send())
@@ -1560,15 +1572,13 @@
         sib_send(u, u % 2).wait_send()
     for u in finals[-2:]:
         fin_wait(u)
-    for j in range(8):
-        unit = (1 - core) * 8 + j
-        remote(
-            fin.at[j % 2],
-            grad_out.at[twin_block(j)],
-            fin_send.at[unit],
-            fin_recv.at[unit],
-            place.twin(),
-        ).wait_recv()
+    for layer in range(2):
+
+        @pl.when(core == layer)
+        def _(layer=layer):
+            for u in range((1 - layer) * 8, (2 - layer) * 8):
+                fin_remote(u, 1 - layer).wait_recv()
+
     give_done(dxb, dx_out, 0)
     give_done(deb, de_out, 3)
 
@@ -1586,7 +1596,13 @@
         out_shape=(
             shape((2 * SEQ, D), HALF),
             shape((2 * SEQ, D), HALF),
-            shape((16, rank, D), FULL),
+            shape((rank, 3 * D), FULL),
+            shape((rank, D), FULL),
+            shape((rank, 2 * D), FULL),
+            shape((rank, D), FULL),
+            shape((rank, D), FULL),
+            shape((4, rank, D), FULL),
+            shape((4 * rank, D), FULL),
             shape((2, 8, D), FULL),
             shape((SEQ, D), HALF),
             shape((16,) + dims + (rank, D), HALF),
@@ -1595,7 +1611,7 @@
             shape((16, DEEP_SLOTS, wide, rank, D), HALF),
         ),
         in_specs=[pl.BlockSpec(memory_space=pltpu.SMEM)] + [anyw] * 8 + [vmem] * 2,
-        out_specs=(anyw, anyw, anyw, vmem) + (anyw,) * 5,
+        out_specs=(anyw,) * 9 + (vmem,) + (anyw,) * 5,
         scratch_shapes=[
             pltpu.VMEM((SLOTS + 2,) + dims + (rank, D), HALF),
             pltpu.VMEM((4,) + dims + (rank, D), HALF),
@@ -1670,25 +1686,22 @@
     meta = jnp.stack([lengths, seq_types, jnp.sum(enc_mask, 1)])
     w_all, outs, *saved = run_forward(dims, meta, pack, small, inputs, encoder[0])
     grads = run_backward(dims, meta, cotangent[0], w_all, saved)
-    d_in, d_mem, blocks, sums = grads[:4]
-
-    def columns(first, last):
-        return jnp.moveaxis(blocks[first:last], 0, 1).reshape(1, rank, -1)
-
-    inner = blocks[8:12].reshape(4, rank, chips, rank).transpose(1, 2, 0, 3)
+    d_in, d_mem, d_qkv, d_out, d_kv, d_cq, d_co, inner, outer, sums = grads[:10]
+
+    inner = inner.reshape(4, rank, chips, rank).transpose(1, 2, 0, 3)
     own = lax.dynamic_index_in_dim(sums, lax.axis_index("section"), 0, keepdims=False)
     own = lax.dynamic_slice_in_dim(own, lax.axis_index("dp") * rank, rank, 1)
     return (
         outs[None],
         d_in[None],
         d_mem[None],
-        columns(0, 3),
-        blocks[3:4],
-        blocks[6:7],
-        columns(4, 6),
-        blocks[7:8],
+        d_qkv[None],
+        d_out[None],
+        d_cq[None],
+        d_kv[None],
+        d_co[None],
         inner.reshape(1, rank, 4 * D),
-        blocks[12:16].reshape(1, 4 * rank, D),
+        outer[None],
         own[None, :3],
         own[None, 3:5],
     )

time: 682 us -> 676 us (level)
  no operation moved by 1% of the time
where the time goes in v3:
time: 676 us; the launch traced here: 671 us
  Pallas kernels  637 us (94%)
  local copies, waits for them, and re-layouts  24 us (4%)
  other arithmetic  8.83 us (1%)
    pallas_call x1, Pallas kernels, run_forward(): pl.pallas_call(functools.partial(forward_kernel, dims), out_shape=(shape(...  324 us
    pallas_call x1, Pallas kernels, run_backward(): pl.pallas_call(functools.partial(backward_kernel, dims), out_shape=(shape...  313 us

profile of v3, /device:TPU:0, one launch (start us, length us, event | category | flops | bytes accessed | tf_op | source)
XLA Modules:
  0.0 671.2 jit_solution(170173769790884126)
XLA Ops:
  0.7 0.9 reduce_sum.9
  1.5 1.3 pad_add_fusion.meta
  2.8 1.3 convert_element_type.58
  4.2 1.1 convert_element_type.57
  5.5 0.7 stack_reshape.4
  6.2 1.0 convert_element_type.51
  8.0 1.0 convert_element_type.55
  9.0 1.0 convert_element_type.54
  10.4 1.6 pad_maximum_fusion.pack
  12.6 324.0 %shard_map.238 = (bf16[32,4,2,2,64,1024]{5,4,3,2,1,0:T(8,128)(2,1)}, bf16[1024,1024]{1,0:T(8,128)(2,1)}, bf16[2,6,512,1024]{3,2,1,0:T(8,128)(2,1)}, bf16[2,6,102...) custom-call(s32[3,2]{1,0:T(4,128)} %pad_add_fusion.meta, ...), custom_call_target="tpu_custom_call" | custom-call | flops 40000000000 | bytes 300000000 | tf_op jit(solution)/shard_map/pallas_call | solution.py:692
  336.6 313.3 %shard_map.239 = (bf16[1024,1024]{1,0:T(8,128)(2,1)}, bf16[1024,1024]{1,0:T(8,128)(2,1)}, f32[64,3072]{1,0:T(8,128)}, f32[64,1024]{1,0:T(8,128)}, f32[64,2048]{1...) custom-call(s32[3,2]{1,0:T(4,128)} %pad_add_fusion.meta, ...), custom_call_target="tpu_custom_call" | custom-call | flops 80000000000 | bytes 400000000 | tf_op jit(solution)/shard_map/pallas_call | solution.py:1594
  649.9 1.7 reshape.55
  651.6 2.7 copy.35
  654.3 3.7 reshape.56
  658.0 0.8 constant_dynamic-slice_fusion
  659.9 1.3 copy.56
  661.2 1.0 copy-done.2
  662.3 1.3 copy.57
  663.6 1.0 copy-done.1
  664.6 1.3 copy.58
  666.3 0.9 copy.59
  667.2 0.7 copy.60
  668.6 0.8 copy.62
  670.1 1.0 copy.64
  (43 shorter events, 4.9 us)
Async XLA Ops:
  0.6 3.5 copy-start.3
  5.3 1.9 copy-start.5
  6.2 3.8 copy-start.7
  10.4 1.6 copy-start.13
  10.4 1.6 copy-start.12
  654.3 5.6 copy-start
  659.9 2.3 copy-start.2
  662.3 2.3 copy-start.1
  664.6 1.7 copy-start.6
  664.6 2.5 copy-start.11
  664.6 3.2 copy-start.10
  666.3 2.3 copy-start.8
  666.3 3.1 copy-start.9
  666.3 3.8 copy-start.4
